TPU v7x, 32 devices: a whole 2x2x4 slice. The times are simulated.
32 devices in a mesh: grp: 2 (over y), pencil: 4 (over z), depth: 2 (over x), mem: 2 (over core).
Axes of the slice: x: 2, y: 2, z: 4, core: 2. Of those that a mesh axis runs over, the one named last changes fastest.
Arguments:
- density: float32 [4, 2, 2048, 2048], P(('grp', 'mem'), 'depth', 'pencil'), parts along dimension 0, may hold values from -6 to 6
- background: float32 [8, 2], P(None, 'depth'), may hold values from -2 to 2
- member_ids: int32 [4], P(('grp', 'mem')), parts along dimension 0, may hold values from 0 to 7
- layer_kernel: int32 [2], P('depth'), may hold values from 0 to 3, as said below
- kernel_spectra: bfloat16 [4, 2, 2048, 2048], P('depth', None, None, 'pencil'), may hold values from -4 to 4
Outputs:
- gravity: float32 [4, 2048, 2048], P(('grp', 'mem'), ('pencil', 'depth')), parts along dimension 0
There are 2 independent parts, one for each index of `grp`. A program takes and returns all parts, laid end to end along the dimension named above; an argument that names none is the same for every part. Nothing has to cross between parts.
Inputs may be any that keep to these rules, and one draw needn't show every extreme that they name: Layer l takes one of the 2 kernels of its depth band: layer_kernel[l] // 2 equals l.
All inputs are finite; a program needn't handle non-finite values.
Results may differ from a plain program's by a relative error of at most 0.0003.
Values sent between devices are 32-bit elements; how exact they have to be, the bound alone decides.
A program may use at most 128 MiB of HBM per device.

v0:
```python
import math

import jax
import jax.numpy as jnp
from jax import lax
from jax.sharding import PartitionSpec as P

base_radix = 16
highest = lax.Precision.HIGHEST


def twiddle_table(row_count, col_count, modulus):
    left_index = lax.broadcasted_iota(jnp.int32, (row_count, col_count), 0)
    right_index = lax.broadcasted_iota(jnp.int32, (row_count, col_count), 1)
    angles = (left_index * right_index % modulus).astype(jnp.float32) * (2.0 * math.pi / modulus)
    return (jnp.cos(angles), jnp.sin(angles))


def forward_rows(values):
    leading = values.shape[:-1]
    length = values.shape[-1]
    inner_len = length // base_radix
    blocks = values.reshape(leading + (base_radix, inner_len))
    cos_small, sin_small = twiddle_table(base_radix, base_radix, base_radix)
    first_real = jnp.einsum("kn,...nm->...km", cos_small, blocks, precision=highest)
    first_imag = -jnp.einsum("kn,...nm->...km", sin_small, blocks, precision=highest)
    cos_turn, sin_turn = twiddle_table(base_radix, inner_len, length)
    turned_real = first_real * cos_turn + first_imag * sin_turn
    turned_imag = first_imag * cos_turn - first_real * sin_turn
    cos_large, sin_large = twiddle_table(inner_len, inner_len, inner_len)
    final_real = jnp.einsum(
        "...kn,nm->...km", turned_real, cos_large, precision=highest
    ) + jnp.einsum("...kn,nm->...km", turned_imag, sin_large, precision=highest)
    final_imag = jnp.einsum(
        "...kn,nm->...km", turned_imag, cos_large, precision=highest
    ) - jnp.einsum("...kn,nm->...km", turned_real, sin_large, precision=highest)
    return (final_real.reshape(leading + (length,)), final_imag.reshape(leading + (length,)))


def forward_columns(real_part, imag_part):
    leading = real_part.shape[:-2]
    length = real_part.shape[-2]
    col_width = real_part.shape[-1]
    inner_len = length // base_radix
    block_shape = leading + (base_radix, inner_len, col_width)
    split_real = real_part.reshape(block_shape)
    split_imag = imag_part.reshape(block_shape)
    cos_small, sin_small = twiddle_table(base_radix, base_radix, base_radix)
    first_real = jnp.einsum(
        "kn,...nmq->...kmq", cos_small, split_real, precision=highest
    ) + jnp.einsum("kn,...nmq->...kmq", sin_small, split_imag, precision=highest)
    first_imag = jnp.einsum(
        "kn,...nmq->...kmq", cos_small, split_imag, precision=highest
    ) - jnp.einsum("kn,...nmq->...kmq", sin_small, split_real, precision=highest)
    cos_turn, sin_turn = twiddle_table(base_radix, inner_len, length)
    cos_turn = cos_turn[:, :, None]
    sin_turn = sin_turn[:, :, None]
    turned_real = first_real * cos_turn + first_imag * sin_turn
    turned_imag = first_imag * cos_turn - first_real * sin_turn
    cos_large, sin_large = twiddle_table(inner_len, inner_len, inner_len)
    final_real = jnp.einsum(
        "...kmq,mj->...kjq", turned_real, cos_large, precision=highest
    ) + jnp.einsum("...kmq,mj->...kjq", turned_imag, sin_large, precision=highest)
    final_imag = jnp.einsum(
        "...kmq,mj->...kjq", turned_imag, cos_large, precision=highest
    ) - jnp.einsum("...kmq,mj->...kjq", turned_real, sin_large, precision=highest)
    out_shape = leading + (length, col_width)
    return (final_real.reshape(out_shape), final_imag.reshape(out_shape))


def inverse_columns(real_part, imag_part):
    length = real_part.shape[0]
    col_width = real_part.shape[1]
    inner_len = length // base_radix
    split_real = real_part.reshape(base_radix, inner_len, col_width)
    split_imag = imag_part.reshape(base_radix, inner_len, col_width)
    cos_large, sin_large = twiddle_table(inner_len, inner_len, inner_len)
    first_real = jnp.einsum("kmq,mj->kjq", split_real, cos_large, precision=highest) - jnp.einsum(
        "kmq,mj->kjq", split_imag, sin_large, precision=highest
    )
    first_imag = jnp.einsum("kmq,mj->kjq", split_imag, cos_large, precision=highest) + jnp.einsum(
        "kmq,mj->kjq", split_real, sin_large, precision=highest
    )
    cos_turn, sin_turn = twiddle_table(base_radix, inner_len, length)
    cos_turn = cos_turn[:, :, None]
    sin_turn = sin_turn[:, :, None]
    turned_real = first_real * cos_turn - first_imag * sin_turn
    turned_imag = first_imag * cos_turn + first_real * sin_turn
    cos_small, sin_small = twiddle_table(base_radix, base_radix, base_radix)
    final_real = jnp.einsum("nk,kjq->njq", cos_small, turned_real, precision=highest) - jnp.einsum(
        "nk,kjq->njq", sin_small, turned_imag, precision=highest
    )
    final_imag = jnp.einsum("nk,kjq->njq", cos_small, turned_imag, precision=highest) + jnp.einsum(
        "nk,kjq->njq", sin_small, turned_real, precision=highest
    )
    return (final_real.reshape(length, col_width), final_imag.reshape(length, col_width))


def inverse_rows(real_part, imag_part):
    row_count = real_part.shape[0]
    length = real_part.shape[1]
    inner_len = length // base_radix
    split_real = real_part.reshape(row_count, base_radix, inner_len)
    split_imag = imag_part.reshape(row_count, base_radix, inner_len)
    cos_large, sin_large = twiddle_table(inner_len, inner_len, inner_len)
    first_real = jnp.einsum("rkm,mj->rkj", split_real, cos_large, precision=highest) - jnp.einsum(
        "rkm,mj->rkj", split_imag, sin_large, precision=highest
    )
    first_imag = jnp.einsum("rkm,mj->rkj", split_imag, cos_large, precision=highest) + jnp.einsum(
        "rkm,mj->rkj", split_real, sin_large, precision=highest
    )
    cos_turn, sin_turn = twiddle_table(base_radix, inner_len, length)
    turned_real = first_real * cos_turn - first_imag * sin_turn
    turned_imag = first_imag * cos_turn + first_real * sin_turn
    cos_small, sin_small = twiddle_table(base_radix, base_radix, base_radix)
    final_real = jnp.einsum("nk,rkj->rnj", cos_small, turned_real, precision=highest) - jnp.einsum(
        "nk,rkj->rnj", sin_small, turned_imag, precision=highest
    )
    return final_real.reshape(row_count, length)


def body(density, background, member_ids, layer_kernel, kernel_spectra):
    profiles = background.shape[0]
    chosen = (lax.broadcasted_iota(jnp.int32, (profiles,), 0) == member_ids[0]).astype(jnp.float32)
    offsets = jnp.dot(chosen, background, precision=highest)
    contrast = density[0] - offsets[:, None, None]
    row_real, row_imag = forward_rows(contrast)
    paired = jnp.stack([row_real, row_imag], axis=1)
    layer_block = lax.all_to_all(paired, "pencil", split_axis=3, concat_axis=2, tiled=True)
    out_real, out_imag = forward_columns(layer_block[:, 0], layer_block[:, 1])
    spectra = jnp.stack([out_real, out_imag], axis=1)
    kern_count = kernel_spectra.shape[0]
    layer_count = layer_kernel.shape[0]
    band_start = lax.axis_index("depth") * kern_count
    local_index = layer_kernel - band_start
    weights = (
        local_index[:, None] == lax.broadcasted_iota(jnp.int32, (layer_count, kern_count), 1)
    ).astype(jnp.float32)
    binned = jnp.einsum("lk,lcxq->kcxq", weights, spectra, precision=highest)
    kernels = kernel_spectra.astype(jnp.float32)
    part_real = jnp.sum(binned[:, 0] * kernels[:, 0] - binned[:, 1] * kernels[:, 1], axis=0)
    part_imag = jnp.sum(binned[:, 0] * kernels[:, 1] + binned[:, 1] * kernels[:, 0], axis=0)
    partial_value = jnp.stack([part_real, part_imag], axis=0)
    depth_count = lax.axis_size("depth")
    pencil_count = lax.axis_size("pencil")
    length_x = partial_value.shape[1]
    col_width = partial_value.shape[2]
    rows_out = length_x // (pencil_count * depth_count)
    summed = lax.psum(partial_value, "depth")
    field_real, field_imag = inverse_columns(summed[0], summed[1])
    stacked = jnp.stack([field_real, field_imag], axis=1)
    own_rows = lax.dynamic_index_in_dim(
        stacked.reshape(pencil_count, depth_count, rows_out, 2, col_width),
        lax.axis_index("depth"),
        1,
        keepdims=False,
    )
    gathered = lax.all_to_all(own_rows, "pencil", split_axis=0, concat_axis=3, tiled=True)
    grid_rows = gathered[0]
    result = inverse_rows(grid_rows[:, 0], grid_rows[:, 1]) * (
        1.0 / (length_x * grid_rows.shape[-1])
    )
    return result[None]


def solution(mesh):
    placed = (
        P(("grp", "mem"), "depth", "pencil", None),
        P(None, "depth"),
        P(("grp", "mem")),
        P("depth"),
        P("depth", None, None, "pencil"),
    )
    return jax.shard_map(
        body,
        mesh=mesh,
        in_specs=placed,
        out_specs=P(("grp", "mem"), ("pencil", "depth"), None),
        check_vma=False,
    )
```

profile of v0, /device:TPU:0, one launch (start us, length us, event | category | flops | bytes accessed | tf_op | source)
XLA Modules:
  0.0 762.8 jit_solution(689112349098130173)
XLA Ops:
  32.9 6.1 fusion.43
  44.8 8.0 %copy.122 = f32[1,1,512,2048]{2,1,0,3:T(1,128)S(1)} copy(f32[1,1,512,2048]{2,3,1,0:T(8,128)S(1)} %bitcast.222) | data formatting | bytes 8388608 | tf_op jit(solution)/shard_map/stack;reshape | solution.py:128
  52.8 8.0 %copy.121 = f32[1,1,512,2048]{2,1,0,3:T(1,128)S(1)} copy(f32[1,1,512,2048]{2,3,1,0:T(8,128)S(1)} %bitcast.221) | data formatting | bytes 8388608 | tf_op jit(solution)/shard_map/stack;reshape | solution.py:128
  60.8 8.8 %pad_maximum_fusion = f32[1,2,512,2048]{2,1,0,3:T(2,128)} fusion(f32[1,1,512,2048]{2,1,0,3:T(1,128)S(1)} %copy.122, f32[1,1,512,2048]{2,1,0,3:T(1,128)S(1)} %copy.121), kind=kLoop, calls=%fused_computation | loop fusion | flops 2097152 | bytes 16777216 | tf_op jit(solution)/shard_map/stack | solution.py:128
  69.6 6.3 all-to-all-start
  76.8 11.5 %convert_element_type.136 = f32[2,2,2048,512]{3,2,1,0:T(8,128)} convert(bf16[2,2,2048,512]{3,2,1,0:T(8,128)(2,1)} %param.9) | non-fusion elementwise | flops 4194304 | bytes 25165824 | tf_op jit(solution)/shard_map/convert_element_type | solution.py:140
  88.3 171.7 %all-to-all-done = f32[1,2,512,2048]{2,1,0,3:T(2,128)} async-done(((f32[1,2,512,2048]{2,1,0,3:T(2,128)}), f32[1,2,512,2048]{2,1,0,3:T(2,128)}, u32[]{:S(2)}, u32[]{:S(2)}) %all-to-all-start) | async-done | bytes 8388640 | tf_op jit(solution)/shard_map/all_to_all | solution.py:129
  260.0 8.2 %copy.123 = f32[1,2,512,2048]{2,3,1,0:T(8,128)} copy(f32[1,2,512,2048]{2,1,0,3:T(2,128)} %all-to-all-done) | data formatting | bytes 16777216 | tf_op jit(solution)/shard_map/all_to_all | solution.py:129
  268.2 10.0 %copy.124 = f32[1,2,4,512,512]{4,3,2,1,0:T(8,128)} copy(f32[1,2,4,512,512]{3,4,2,1,0:T(8,128)} %bitcast.216) | data formatting | bytes 16777216 | tf_op jit(solution)/shard_map/all_to_all | solution.py:129
  282.7 6.8 fusion.27
  289.5 6.8 fusion.29
  296.3 7.2 fusion.49
  303.5 8.9 %fusion.4 = (f32[16,128,512]{2,0,1:T(8,128)S(1)}, f32[16,128,512]{2,0,1:T(8,128)S(1)}) fusion(f32[128,512,16]{1,2,0:T(8,128)S(1)} %fusion.49, f32[16,128]{0,1:T(8,128)S(1)} %copy.130, f32[16,128]{0,1:T(8,128)S(1)} %copy.127, f32[128,512,16]{1,2,0:T(8,128)S(1)} %fusion.27, f32[16,128,512]{2,1,0:T(8,128)S(1)} %bitcast.206), kind=kOutput, calls=%fused_computation.18 | convolution fusion | flops 208670208 | bytes 20987904 | tf_op jit(solution)/shard_map/kn,...nmq->...kmq/dot_general | solution.py:54
  312.4 6.1 fusion.19
  318.5 6.5 fusion.21
  325.1 6.4 fusion.55
  331.5 6.7 fusion.58
  342.4 11.4 %broadcast_multiply_fusion = f32[2,2,2048,512]{3,2,1,0:T(8,128)} fusion(f32[2,2048,512]{2,1,0:T(8,128)} %maximum_bitcast_fusion, f32[2]{0:T(128)S(1)} %fusion.159), kind=kLoop, calls=%fused_computation.7 | loop fusion | flops 4194304 | bytes 25165832 | tf_op jit(solution)/shard_map/lk,lcxq->kcxq/dot_general | solution.py:139
  353.8 17.3 %subtract_reduce_fusion = (f32[2048,512]{1,0:T(8,128)}, f32[2048,512]{1,0:T(8,128)}) fusion(f32[2,2,2048,512]{3,2,1,0:T(8,128)} %convert_element_type.136, f32[2,2,2048,512]{3,2,1,0:T(8,128)} %broadcast_multiply_fusion), kind=kLoop, calls=%fused_computation.6 | loop fusion | flops 14680064 | bytes 41943040 | tf_op jit(solution)/shard_map/reduce_sum | solution.py:141
  371.1 7.7 %pad_maximum_fusion.1 = f32[2,2048,512]{2,1,0:T(8,128)} fusion(f32[1,2048,512]{2,1,0:T(8,128)} %bitcast.225, f32[1,2048,512]{2,1,0:T(8,128)} %bitcast.224), kind=kLoop, calls=%fused_computation.2 | loop fusion | flops 2097152 | bytes 16777216 | tf_op jit(solution)/shard_map/stack | solution.py:143
  378.8 197.3 %all-reduce.2.cloned.1.call-done = f32[2,2048,512]{2,1,0:T(8,128)} async-done(((f32[2,2048,512]{2,1,0:T(8,128)}), f32[2,2048,512]{2,1,0:T(8,128)}) %all-reduce.2.cloned.1.call-update) | async-done | bytes 8388624 | tf_op jit(solution)/shard_map/psum | solution.py:149
  598.9 6.0 fusion.11
  610.5 6.1 fusion.61
  627.8 97.6 %all_to_all.33 = f32[4,256,2,512]{3,1,2,0:T(8,128)} all-to-all(f32[4,256,2,512]{3,1,2,0:T(8,128)S(1)} %copy_bitcast_fusion), channel_id=1, replica_groups=mesh['grp'=2,'pencil'=4,'depth'=2,'mem'=2] {'pencil'}, dimensions={0} | all-to-all | bytes 8388608 | tf_op jit(solution)/shard_map/all_to_all | solution.py:158
  (35 shorter events, 110.1 us)
Async XLA Ops:
  69.6 190.4 %all-to-all-start = ((f32[1,2,512,2048]{2,1,0,3:T(2,128)}), f32[1,2,512,2048]{2,1,0,3:T(2,128)}, u32[]{:S(2)}, u32[]{:S(2)}) async-start(f32[1,2,512,2048]{2,1,0,3:T(2,128)} %pad_maximum_fusion), calls=%async_computation | async-start | bytes 16777216 | tf_op jit(solution)/shard_map/all_to_all | solution.py:129
  75.9 500.2 %all-reduce.2.cloned.1.call-start = ((), (), s32[]{:S(2)}) async-start(), calls=%async_computation.2 | async-start | bytes 16777216 | tf_op jit(solution)/shard_map/psum | solution.py:149
Sparse Core Ops, SparseCore 0:
  378.9 197.1 all-reduce.1
where the time goes:
time: 772 us; the launch traced here: 763 us
  waiting for transfers between devices  369 us (48%)
  matrix products  150 us (19%)
  blocking collectives  97.6 us (13%)
  other arithmetic  66 us (9%)
  local copies, waits for them, and re-layouts  58.4 us (8%)
  between operations  15.2 us (2%)
    psum x1, waiting for transfers between devices, body(): summed = lax.psum(partial_value, 'depth')  197 us
    all_to_all x1, waiting for transfers between devices, body(): lax.all_to_all(paired, 'pencil', split_axis=3, concat_axis=2, tiled=True)  172 us
    all_to_all x1, blocking collectives, body(): lax.all_to_all(own_rows, 'pencil', split_axis=0, concat_axis=3, tiled=True)  97.6 us
    all_to_all x2, local copies, waits for them, and re-layouts, body(): lax.all_to_all(paired, 'pencil', split_axis=3, concat_axis=2, tiled=True)  18.2 us
    reduce_sum x1, other arithmetic, body(): jnp.sum(binned[:, 0] * kernels[:, 0] - binned[:, 1] * kernels[:, 1], axis=0)  17.3 us
    another operation x2, local copies, waits for them, and re-layouts, body(): paired = jnp.stack([row_real, row_imag], axis=1)  16 us
  transfers between devices with their start and end apart: 2, of which 2 were waited for; matrix products, arithmetic and copies ran while one was open for 2% of the time, Pallas kernels for 0%

commit v1 on v0

v1 whole, which is shorter than its diff:
```python
import functools
import math

import jax
import jax.numpy as jnp
import numpy as np
from jax import lax
from jax.experimental import pallas as pl
from jax.experimental.pallas import tpu as pltpu
from jax.sharding import PartitionSpec as P

RADIX = 16
INNER = 128
HALF = 64
LENGTH = RADIX * INNER
f32 = jnp.float32
bf16 = jnp.bfloat16


def halves(table):
    table = np.asarray(table, np.float32)
    high = table.astype(bf16)
    low = (table - high.astype(np.float32)).astype(bf16)
    return jnp.asarray(high), jnp.asarray(low)


def residue_rows(r):
    m = np.arange(INNER)[:, None]
    q = np.arange(HALF)[None, :]
    turn = np.exp(-2j * np.pi * (((RADIX * q + r) * m) % LENGTH) / LENGTH)
    re, im = turn.real.copy(), turn.imag.copy()
    if r == 0:
        im[:, 0] = (-1.0) ** m[:, 0]
    out = np.zeros((2 * INNER, 2 * HALF))
    if r == 0:
        out[:INNER, :HALF], out[:INNER, HALF:] = re, im
    elif r == 8:
        out[INNER:, :HALF], out[INNER:, HALF:] = re, im
    else:
        sign = 1.0 if r < 8 else -1.0
        out[:INNER, :HALF], out[:INNER, HALF:] = re, im
        out[INNER:, :HALF], out[INNER:, HALF:] = -sign * im, sign * re
    return out


def slot_of(r):
    return 0 if r in (0, 8) else min(r, RADIX - r)


def row_tables():
    tables = np.zeros((8, 512, 256))
    for t in range(8):
        for odd in range(2):
            block = residue_rows(2 * t + odd)
            rows = slice(256 * odd, 256 * odd + 256)
            tables[t, rows, HALF * odd : HALF * odd + HALF] = block[:, :HALF]
            tables[t, rows, 128 + HALF * odd : 128 + HALF * odd + HALF] = block[:, HALF:]
    return tables


def inverse_row_tables():
    tables = np.zeros((8, 512, 256))
    scale = 1.0 / (LENGTH * LENGTH)
    for s in range(8):
        for place, r in enumerate((s, 8 if s == 0 else RADIX - s)):
            block = residue_rows(r).T.copy() * scale
            weight = np.full((2 * HALF, 1), 2.0 if r in (0, 8) else 1.0)
            if r == 0:
                weight[0] = weight[HALF] = 1.0
            block *= weight
            odd = r % 2
            tables[s, 256 * place + HALF * odd : 256 * place + HALF * odd + HALF] += block[:HALF]
            tables[s, 256 * place + 128 + HALF * odd : 256 * place + 128 + HALF * odd + HALF] += block[HALF:]
    return tables


def column_tables():
    q = np.arange(INNER)[:, None]
    m = np.arange(INNER)[None, :]
    tables = np.zeros((RADIX, 256, 256))
    for r in range(RADIX):
        turn = np.exp(-2j * np.pi * (((RADIX * q + r) * m) % LENGTH) / LENGTH)
        tables[r] = np.block([[turn.real, -turn.imag], [turn.imag, turn.real]])
    return tables


def split_value(value):
    high = value.astype(bf16)
    return high, (value - high.astype(f32)).astype(bf16)


def dot(a, b):
    return jnp.dot(a, b, preferred_element_type=f32)


def rotate(value, count, length, sign):
    re, im = value
    count %= length
    if count == 0:
        return value
    if 4 * count == length:
        return (im, -re) if sign < 0 else (-im, re)
    c = math.cos(2 * math.pi * count / length)
    s = sign * math.sin(2 * math.pi * count / length)
    if 8 * count == length:
        return ((re + im) * c, (im - re) * c) if sign < 0 else ((re - im) * c, (im + re) * c)
    return (re * c - im * s, re * s + im * c)


def plus(a, b):
    return (a[0] + b[0], a[1] + b[1])


def minus(a, b):
    return (a[0] - b[0], a[1] - b[1])


def transform(values, sign):
    length = len(values)
    if length == 1:
        return values
    even, odd = transform(values[0::2], sign), transform(values[1::2], sign)
    turned = [rotate(odd[k], k, length, sign) for k in range(length // 2)]
    return [plus(even[k], turned[k]) for k in range(length // 2)] + [
        minus(even[k], turned[k]) for k in range(length // 2)
    ]


def real_transform(values):
    length = len(values)
    if length == 2:
        return [(values[0] + values[1], None), (values[0] - values[1], None)]
    even, odd = real_transform(values[0::2]), real_transform(values[1::2])
    out = [None] * (length // 2 + 1)
    out[0] = (even[0][0] + odd[0][0], None)
    out[length // 2] = (even[0][0] - odd[0][0], None)
    quarter = length // 4
    for k in range(1, quarter):
        turned = rotate(odd[k], k, length, -1)
        out[k] = plus(even[k], turned)
        low = minus(even[k], turned)
        out[length // 2 - k] = (low[0], -low[1])
    out[quarter] = (even[quarter][0], -odd[quarter][0])
    return out


def real_inverse(values):
    half = len(values) - 1
    length = 2 * half
    if length == 2:
        return [values[0][0] + values[1][0], values[0][0] - values[1][0]]
    even, odd = [], []
    for k in range(half // 2 + 1):
        if k == 0:
            even.append((values[0][0] + values[half][0], None))
            odd.append((values[0][0] - values[half][0], None))
        elif k == half // 2:
            even.append((2.0 * values[k][0], None))
            odd.append((-2.0 * values[k][1], None))
        else:
            other = values[half - k]
            even.append((values[k][0] + other[0], values[k][1] - other[1]))
            odd.append(rotate((values[k][0] - other[0], values[k][1] + other[1]), k, length, 1))
    first, second = real_inverse(even), real_inverse(odd)
    return [x for pair in zip(first, second) for x in pair]


def rows_kernel(pencils, width, offset_ref, in_ref, high_ref, low_ref, *rest):
    outs, pieces = rest[:-1], rest[-1]
    rows = in_ref.shape[0]
    per = RADIX // pencils
    offset = offset_ref[0]

    def step(b, carry):
        at = pl.ds(pl.multiple_of(b * 8, 8), 8)
        values = [in_ref[at, n * INNER : (n + 1) * INNER] - offset for n in range(RADIX)]
        got = real_transform(values)
        pieces[0, at, :INNER] = got[0][0]
        pieces[0, at, INNER:] = got[8][0]
        for s in range(1, 8):
            pieces[s, at, :INNER] = got[s][0]
            pieces[s, at, INNER:] = got[s][1]
        return carry

    lax.fori_loop(0, rows // 8, step, 0)
    for t in range(8):
        total = None
        for odd in range(2):
            high, low = split_value(pieces[slot_of(2 * t + odd)])
            table_high = high_ref[t, 256 * odd : 256 * odd + 256]
            table_low = low_ref[t, 256 * odd : 256 * odd + 256]
            part = dot(high, table_high) + dot(low, table_high) + dot(high, table_low)
            total = part if total is None else total + part
        if width == 2:
            pencil, place = divmod(2 * t, per)
            for c in range(2):
                outs[place // 2][pencil, c] = total[:, c * 128 : (c + 1) * 128]
        else:
            for odd in range(2):
                pencil, place = divmod(2 * t + odd, per)
                for c in range(2):
                    begin = c * 128 + odd * HALF
                    outs[place][pencil, c] = total[:, begin : begin + HALF]


def columns_kernel(special, mine_ref, in_ref, kern_ref, mirror_ref, swap_ref, fh_ref, fl_ref, ih_ref, il_ref,
                   out_ref, pieces, waves):
    part_rows = in_ref.shape[2]
    depths, pencils, _, out_rows, _ = out_ref.shape
    mine = mine_ref[0]

    def forward(b, carry):
        values = []
        for n in range(RADIX):
            source, begin = divmod(n * INNER, part_rows)
            at = pl.ds(pl.multiple_of(begin + b * 8, 8), 8)
            values.append((in_ref[source, 0, at, :], in_ref[source, 1, at, :]))
        at = pl.ds(pl.multiple_of(b * 8, 8), 8)
        also = pl.ds(pl.multiple_of(INNER + b * 8, 8), 8)
        for r, (re, im) in enumerate(transform(values, -1)):
            pieces[r, at, :] = re
            pieces[r, also, :] = im
        return carry

    lax.fori_loop(0, INNER // 8, forward, 0)

    def wave(r):
        high, low = split_value(pieces[r])
        return dot(fh_ref[r], high) + dot(fh_ref[r], low) + dot(fl_ref[r], high)

    def finish(r, got, extra):
        re, im = got[:INNER], got[INNER:]
        kr, ki = kern_ref[0, r], kern_ref[1, r]
        sr, si = re * kr - im * ki, re * ki + im * kr
        if extra is not None:
            sr, si = sr + extra[0], si + extra[1]
        spectrum = jnp.concatenate([sr, si], axis=0)
        high, low = split_value(spectrum)
        pieces[r] = dot(ih_ref[r], high) + dot(ih_ref[r], low) + dot(il_ref[r], high)

    if special:
        for r in range(RADIX):
            waves[r] = wave(r)
        for r in range(RADIX):
            other = (RADIX - r) % RADIX
            high, low = split_value(waves[other])
            swap = swap_ref[0 if r == 0 else 1]
            re = dot(swap, high[:INNER]) + dot(swap, low[:INNER])
            im = -(dot(swap, high[INNER:]) + dot(swap, low[INNER:]))
            kr, ki = mirror_ref[0, r], mirror_ref[1, r]
            finish(r, waves[r], (re * kr - im * ki, re * ki + im * kr))
    else:
        for r in range(RADIX):
            finish(r, wave(r), None)

    def backward(b, carry):
        at = pl.ds(pl.multiple_of(b * 8, 8), 8)
        also = pl.ds(pl.multiple_of(INNER + b * 8, 8), 8)
        values = [(pieces[r, at, :], pieces[r, also, :]) for r in range(RADIX)]
        for n, (re, im) in enumerate(transform(values, 1)):
            x = n * INNER + b * 8
            pencil = x // (out_rows * depths)
            depth = lax.rem(x // out_rows - mine + depths, depths)
            put = pl.ds(pl.multiple_of(lax.rem(x, out_rows), 8), 8)
            out_ref[depth, pencil, 0, put, :] = re
            out_ref[depth, pencil, 1, put, :] = im
        return carry

    lax.fori_loop(0, INNER // 8, backward, 0)


def fields_kernel(pencils, width, *refs):
    chunks = RADIX // pencils // width
    ins, (high_ref, low_ref, out_ref, pieces) = refs[:chunks], refs[chunks:]
    per = RADIX // pencils
    rows = out_ref.shape[1]

    def pair(t):
        if width == 2:
            pencil, place = divmod(2 * t, per)
            ref = ins[place // 2]
            return jnp.concatenate([ref[pencil, 0], ref[pencil, 1]], axis=1)
        found = []
        for c in range(2):
            for odd in range(2):
                pencil, place = divmod(2 * t + odd, per)
                found.append(ins[place][pencil, c])
        return jnp.concatenate(found, axis=1)

    for s in range(8):
        total = None
        for place, r in enumerate((s, 8 if s == 0 else RADIX - s)):
            high, low = split_value(pair(r // 2))
            table_high = high_ref[s, 256 * place : 256 * place + 256]
            table_low = low_ref[s, 256 * place : 256 * place + 256]
            part = dot(high, table_high) + dot(low, table_high) + dot(high, table_low)
            total = part if total is None else total + part
        pieces[s] = total

    def step(b, carry):
        at = pl.ds(pl.multiple_of(b * 8, 8), 8)
        values = [(pieces[0, at, :INNER], None)]
        for s in range(1, 8):
            values.append((pieces[s, at, :INNER], pieces[s, at, INNER:]))
        values.append((pieces[0, at, INNER:], None))
        for n, value in enumerate(real_inverse(values)):
            out_ref[0, at, n * INNER : (n + 1) * INNER] = value
        return carry

    lax.fori_loop(0, rows // 8, step, 0)


def params(**more):
    return pltpu.CompilerParams(vmem_limit_bytes=48 * 1024 * 1024, **more)


def body(density, background, member_ids, layer_kernel, kernel_spectra):
    pencils = lax.axis_size("pencil")
    depths = lax.axis_size("depth")
    sharers = lax.axis_size("grp") * lax.axis_size("mem")
    pencil = lax.axis_index("pencil")
    per = RADIX // pencils
    width = min(per, 2)
    chunks = per // width
    lanes = width * HALF
    part_rows = density.shape[2]
    out_rows = part_rows // depths
    vmem = pl.BlockSpec(memory_space=pltpu.VMEM)
    smem = pl.BlockSpec(memory_space=pltpu.SMEM)

    kern_count = kernel_spectra.shape[0]
    local = layer_kernel[0] - lax.axis_index("depth") * kern_count
    kernel = lax.dynamic_index_in_dim(kernel_spectra, local, 0, keepdims=False)
    kernel = kernel.reshape(2, RADIX, INNER, per, INNER)
    share = RADIX // sharers
    first = lax.axis_index(("grp", "mem")) * share
    taken = jnp.stack(
        [
            lax.dynamic_index_in_dim(kernel, lax.rem(RADIX - first - i, RADIX), 1, keepdims=False)
            for i in range(share)
        ],
        axis=0,
    )
    shape = (share, INNER, INNER)
    to = lax.broadcasted_iota(jnp.int32, shape, 1)
    is_zero = (lax.broadcasted_iota(jnp.int32, shape, 0) + first) == 0
    swap_x = (
        lax.broadcasted_iota(jnp.int32, shape, 2) == jnp.where(is_zero, (INNER - to) % INNER, INNER - 1 - to)
    ).astype(bf16)
    shape = (per, INNER, HALF)
    to = lax.broadcasted_iota(jnp.int32, shape, 2)
    is_zero = (lax.broadcasted_iota(jnp.int32, shape, 0) + pencil) == 0
    swap_y = (
        lax.broadcasted_iota(jnp.int32, shape, 1) == jnp.where(is_zero, (INNER - to) % INNER, INNER - 1 - to)
    ).astype(bf16)
    turned = jnp.einsum("icbjq,jqt->jibct", taken, swap_y, preferred_element_type=bf16)
    turned = turned.reshape(per, share, INNER, 2 * HALF)
    turned = jnp.einsum("iab,jibs->jias", swap_x, turned, preferred_element_type=f32)
    mirrored = lax.ppermute(turned[:1], "pencil", [(p, (pencils - p) % pencils) for p in range(pencils)])
    if per > 1:
        rest = lax.ppermute(
            turned[:0:-1], "pencil", [(p, pencils - 1 - p) for p in range(pencils)]
        )
        mirrored = jnp.concatenate([mirrored, rest], axis=0)
    mirrored = lax.all_gather(mirrored, ("grp", "mem"), axis=1, tiled=True)

    offset = lax.dynamic_index_in_dim(background[:, 0], member_ids[0], 0, keepdims=True)
    row_high, row_low = halves(row_tables())
    block = min(part_rows, 128)
    sent = pl.pallas_call(
        functools.partial(rows_kernel, pencils, width),
        grid=(part_rows // block,),
        in_specs=[
            smem,
            pl.BlockSpec((None, None, block, LENGTH), lambda i: (0, 0, i, 0)),
            pl.BlockSpec((8, 512, 256), lambda i: (0, 0, 0)),
            pl.BlockSpec((8, 512, 256), lambda i: (0, 0, 0)),
        ],
        out_specs=[pl.BlockSpec((pencils, 2, block, lanes), lambda i: (0, 0, i, 0))] * chunks,
        out_shape=[jax.ShapeDtypeStruct((pencils, 2, part_rows, lanes), f32)] * chunks,
        scratch_shapes=[pltpu.VMEM((8, block, 256), f32)],
        compiler_params=params(),
        cost_estimate=pl.CostEstimate(flops=6 * part_rows * 2 * LENGTH * 512, bytes_accessed=12 << 20, transcendentals=0),
    )(offset, density, row_high, row_low)
    arrived = [lax.all_to_all(part, "pencil", 0, 0, tiled=True) for part in sent]

    own = kernel[..., :HALF].astype(f32)
    sign = jnp.array([0.5, -0.5], f32)
    mirrored = mirrored.reshape(per, RADIX, INNER, 2, HALF).transpose(3, 1, 2, 0, 4)
    hermitian = 0.5 * own + sign.reshape(2, 1, 1, 1, 1) * mirrored
    edge = kernel[:, :, :, 0, HALF].astype(f32)
    flipped = jnp.concatenate([edge[:, :1], edge[:, :0:-1]], axis=1)[..., ::-1]
    flipped = jnp.concatenate([jnp.roll(flipped[:, :1], 1, axis=2), flipped[:, 1:]], axis=1)
    edge = 0.5 * edge + sign.reshape(2, 1, 1) * flipped
    zero = hermitian[..., 0, 0]
    both = jnp.where(pencil == 0, 0.5 * (zero + edge), zero)
    apart = jnp.where(pencil == 0, 0.5 * (zero - edge), 0.0)
    place = lax.broadcasted_iota(jnp.int32, (per, HALF), 0) + lax.broadcasted_iota(jnp.int32, (per, HALF), 1)
    hermitian = jnp.where(place == 0, both[..., None, None], hermitian)
    apart = jnp.where(lax.broadcasted_iota(jnp.int32, (lanes,), 0) == 0, apart[..., None], 0.0)

    column = column_tables()
    tables = halves(column) + halves(column.transpose(0, 2, 1))
    index = np.arange(INNER)
    swaps = np.zeros((2, INNER, INNER), np.float32)
    swaps[0, index, (INNER - index) % INNER] = 1.0
    swaps[1, index, INNER - 1 - index] = 1.0
    swaps = jnp.asarray(swaps.astype(bf16))
    two = depths == 2
    mine = lax.axis_index("depth") if two else jnp.int32(0)
    mine = mine.reshape(1)
    fields = []
    for k in range(chunks):
        factors = hermitian[..., k * width : (k + 1) * width, :].reshape(2, RADIX, INNER, lanes)
        special = k == 0
        out = pl.pallas_call(
            functools.partial(columns_kernel, special),
            in_specs=[smem] + [vmem] * 8,
            out_specs=vmem,
            out_shape=jax.ShapeDtypeStruct((depths, pencils, 2, out_rows, lanes), f32),
            scratch_shapes=[
                pltpu.VMEM((RADIX, 256, lanes), f32),
                pltpu.VMEM((RADIX if special else 1, 256, lanes), f32),
            ],
            compiler_params=params(),
            cost_estimate=pl.CostEstimate(flops=12 * RADIX * 256 * 256 * lanes, bytes_accessed=16 << 20, transcendentals=0),
        )(mine, arrived[k], factors, apart if special else apart[:, :1, :8], swaps, *tables)
        if two:
            out = out[0] + lax.ppermute(out[1], "depth", [(0, 1), (1, 0)])
        else:
            out = lax.psum_scatter(out, "depth", scatter_dimension=0, tiled=False)
        fields.append(lax.all_to_all(out, "pencil", 0, 0, tiled=True))

    back_high, back_low = halves(inverse_row_tables())
    return pl.pallas_call(
        functools.partial(fields_kernel, pencils, width),
        in_specs=[vmem] * (chunks + 2),
        out_specs=vmem,
        out_shape=jax.ShapeDtypeStruct((1, out_rows, LENGTH), f32),
        scratch_shapes=[pltpu.VMEM((8, out_rows, 256), f32)],
        compiler_params=params(),
        cost_estimate=pl.CostEstimate(flops=6 * out_rows * 2 * LENGTH * 512, bytes_accessed=8 << 20, transcendentals=0),
    )(*fields, back_high, back_low)


def solution(mesh):
    placed = (
        P(("grp", "mem"), "depth", "pencil", None),
        P(None, "depth"),
        P(("grp", "mem")),
        P("depth"),
        P("depth", None, None, "pencil"),
    )
    return jax.shard_map(
        body,
        mesh=mesh,
        in_specs=placed,
        out_specs=P(("grp", "mem"), ("pencil", "depth"), None),
        check_vma=False,
    )
```

time: 772 us -> 275 us (0.36); the launches traced: 763 us -> 274 us
  waiting for transfers between devices: 369 us -> 79.6 us
  matrix products: 150 us -> 0.93 us
  blocking collectives: 97.6 us -> 28.5 us
  other arithmetic: 66 us -> 9.03 us
  Pallas kernels: 0 us -> 42.2 us
  starting transfers between devices: 6.32 us -> 40.7 us
    psum x1 -> x0, waiting for transfers between devices: 197 us -> none  [body(): summed = lax.psum(partial_value, 'depth')]
    dot_general x28 -> x2, matrix products: 150 us -> 0.93 us  [the longest x1 0.52 us: body(): jnp.einsum('icbjq,jqt->jibct', taken, swap_y, preferred_element_type=bf16)]
    all_to_all x1 -> x3, waiting for transfers between devices: 172 us -> 35.6 us  [the longest x2 35.6 us: body(): lax.all_to_all(part, 'pencil', 0, 0, tiled=True)]
    all_to_all x1, blocking collectives: 97.6 us -> 28.5 us  [body(): fields.append(lax.all_to_all(out, 'pencil', 0, 0, tiled=True))]
    pallas_call x0 -> x4, Pallas kernels: none -> 42.2 us  [the longest x2 28.2 us: body(): pl.pallas_call(functools.partial(columns_kernel, special), in_specs=[smem...]
    ppermute x0 -> x4, waiting for transfers between devices: none -> 40.4 us  [the longest x2 22.6 us: body(): out = out[0] + lax.ppermute(out[1], 'depth', [(0, 1), (1, 0)])]
    all_to_all x1 -> x3, starting transfers between devices: 6.31 us -> 31.9 us  [the longest x2 28.3 us: body(): lax.all_to_all(part, 'pencil', 0, 0, tiled=True)]
    all_to_all x3 -> x0, local copies, waits for them, and re-layouts: 23.5 us -> none  [the longest x2 18.2 us: body(): lax.all_to_all(paired, 'pencil', split_axis=3, concat_axis=2, tiled=True)]
  transfers between devices with their start and end apart: 2 -> 8, of which waited for: 2 -> 5; matrix products, arithmetic and copies ran while one was open for 2% -> 14% of each run, Pallas kernels for 0% -> 13%
where the time goes in v1:
time: 275 us; the launch traced here: 274 us
  waiting for transfers between devices  79.6 us (29%)
  local copies, waits for them, and re-layouts  57.8 us (21%)
  Pallas kernels  42.2 us (15%)
  starting transfers between devices  40.7 us (15%)
  blocking collectives  28.5 us (10%)
  between operations  15 us (5%)
  other arithmetic  9.03 us (3%)
    all_to_all x2, waiting for transfers between devices, body(): lax.all_to_all(part, 'pencil', 0, 0, tiled=True)  35.6 us
    all_to_all x1, blocking collectives, body(): fields.append(lax.all_to_all(out, 'pencil', 0, 0, tiled=True))  28.5 us
    all_to_all x2, starting transfers between devices, body(): lax.all_to_all(part, 'pencil', 0, 0, tiled=True)  28.3 us
    pallas_call x2, Pallas kernels, body(): pl.pallas_call(functools.partial(columns_kernel, special), in_specs=[smem...  28.2 us
    ppermute x2, waiting for transfers between devices, body(): out = out[0] + lax.ppermute(out[1], 'depth', [(0, 1), (1, 0)])  22.6 us
    unnamed x30, local copies, waits for them, and re-layouts  21.4 us
    ppermute x1, waiting for transfers between devices, body(): lax.ppermute(turned[:0:-1], 'pencil', [(p, pencils - 1 - p) for p in rang...  17.8 us
    pallas_call x1, Pallas kernels, body(): pl.pallas_call(functools.partial(rows_kernel, pencils, width), grid=(part...  8.69 us
  transfers between devices with their start and end apart: 8, of which 5 were waited for; matrix products, arithmetic and copies ran while one was open for 14% of the time, Pallas kernels for 13%

profile of v1, /device:TPU:0, one launch (start us, length us, event | category | flops | bytes accessed | tf_op | source)
XLA Modules:
  0.0 273.9 jit_solution(26256211259202457)
XLA Ops:
  7.3 4.4 %constant_dynamic-slice_fusion.4 = bf16[1,2,2048,512]{3,2,1,0:T(8,128)(2,1)} fusion(bf16[2,2,2048,512]{3,2,1,0:T(8,128)(2,1)} %param.19, s32[]{:T(128)S(6)} %select_n.73), kind=kLoop, calls=%fused_computation.64 | loop fusion | bytes 8388612 | tf_op jit(solution)/shard_map/jit(dynamic_index_in_dim)/dynamic_slice | solution.py:333
  11.7 7.0 %reshape.97 = bf16[2,16,128,4,128]{4,3,2,1,0:T(4,128)(2,1)} reshape(bf16[1,2,2048,512]{3,2,1,0:T(8,128)(2,1)} %constant_dynamic-slice_fusion.4) | data formatting | bytes 8388608 | tf_op jit(solution)/shard_map/reshape | solution.py:334
  21.5 5.1 %collective-permute-start.1 = (f32[3,4,128,128]{2,3,0,1:T(8,128)S(1)}, f32[3,4,128,128]{2,3,0,1:T(8,128)S(1)}, u32[]{:S(2)}, u32[]{:S(2)}) collective-permute-start(f32[3,4,128,128]{2,3,0,1:T(8,128)S(1)} %rev.2), channel_id=1, source_target_pairs={{0,12},{4,8},{8,4},{12,0},{1,13},{5,9},{9,5},{13,1},{2,14},{6,10},... | collective-permute-start | bytes 2359304 | tf_op jit(solution)/shard_map/ppermute | solution.py:361
  27.3 17.8 %collective-permute-done.1 = f32[3,4,128,128]{2,3,0,1:T(8,128)S(1)} collective-permute-done((f32[3,4,128,128]{2,3,0,1:T(8,128)S(1)}, f32[3,4,128,128]{2,3,0,1:T(8,128)S(1)}, u32[]{:S(2)}, u32[]{:S(2)}) %collective-permute-start.1) | collective-permute-done | bytes 786464 | tf_op jit(solution)/shard_map/ppermute | solution.py:361
  47.8 8.7 %shard_map.145 = (f32[4,2,512,128]{3,2,1,0:T(8,128)S(1)}, f32[4,2,512,128]{3,2,1,0:T(8,128)S(1)}) custom-call(f32[1]{0:T(128)} %bitcast.2.offset_ref, f32[1,1,512,2048]{3,2,1,0:T(8,128)} %in_ref.1, bf16[8,512,256]{2,1,0:T(8,128)(2,1)} %constant.117.clone.high_ref, bf16[8,512,256]{2,1,0:T(8,128)(2,1)} %constant.118.clone.low_ref), custom_call_target="tpu_custom_call" | custom-call | flops 6442450944 | bytes 12582912 | tf_op jit(solution)/shard_map/pallas_call | solution.py:370
  59.2 24.4 %all-to-all-start.2 = ((f32[4,2,512,128]{3,2,1,0:T(8,128)}), f32[4,2,512,128]{3,2,1,0:T(8,128)S(1)}, u32[]{:S(2)}, u32[]{:S(2)}) async-start(f32[4,2,512,128]{3,2,1,0:T(8,128)} %copy-done.9), calls=%async_computation.2 | async-start | bytes 4194304 | tf_op jit(solution)/shard_map/all_to_all | solution.py:385
  83.6 5.9 %slice.81 = bf16[2,16,128,1,1]{4,3,2,1,0:T(2,128)(2,1)} slice(bf16[2,16,128,4,128]{4,3,2,1,0:T(4,128)(2,1)} %reshape.97), slice={[0:2], [0:16], [0:128], [0:1], [64:65]} | slice | bytes 16384 | tf_op jit(solution)/shard_map/slice | solution.py:391
  89.5 2.8 %copy.82 = bf16[2,16,128,1,1]{2,1,4,3,0:T(8,128)(2,1)S(1)} copy(bf16[2,16,128,1,1]{4,3,2,1,0:T(2,128)(2,1)} %slice.81) | data formatting | bytes 16384
  92.4 5.7 %copy.77 = bf16[2,16,128,4,64]{2,1,0,4,3:T(8,128)(2,1)} copy(bf16[2,16,128,4,64]{4,3,2,1,0:T(4,128)(2,1)} %bitcast.78) | data formatting | bytes 4194304
  98.4 3.6 %all-gather.2.cloned.1.call-done = f32[4,16,128,128]{3,2,0,1:T(8,128)} async-done(((f32[4,4,128,128]{3,2,0,1:T(8,128)}), f32[4,16,128,128]{3,2,0,1:T(8,128)}) %all-gather.2.cloned.1.call-update) | async-done | bytes 4194320 | tf_op jit(solution)/shard_map/all_gather | solution.py:365
  102.0 5.4 %copy.61 = f32[4,16,128,128]{2,3,1,0:T(8,128)} copy(f32[4,16,128,128]{3,2,0,1:T(8,128)} %all-gather.2.cloned.1.call-done) | data formatting | bytes 8388608 | tf_op jit(solution)/shard_map/all_gather | solution.py:365
  107.4 23.6 %all-to-all-done.2.in_ref = f32[4,2,512,128]{3,2,1,0:T(8,128)S(1)} async-done(((f32[4,2,512,128]{3,2,1,0:T(8,128)}), f32[4,2,512,128]{3,2,1,0:T(8,128)S(1)}, u32[]{:S(2)}, u32[]{:S(2)}) %all-to-all-start.2) | async-done | bytes 2097184 | tf_op jit(solution)/shard_map/all_to_all | solution.py:385
  132.3 3.9 %all-to-all-start = ((f32[4,2,512,128]{3,2,1,0:T(8,128)}), f32[4,2,512,128]{3,2,1,0:T(8,128)S(1)}, u32[]{:S(2)}, u32[]{:S(2)}) async-start(f32[4,2,512,128]{3,2,1,0:T(8,128)} %copy-done.8), calls=%async_computation | async-start | bytes 4194304 | tf_op jit(solution)/shard_map/all_to_all | solution.py:385
  136.2 5.4 %bitcast_add_fusion = f32[2,16,128,4,64]{2,1,0,4,3:T(8,128)S(1)} fusion(f32[4,16,128,2,64]{2,4,3,1,0:T(8,128)} %bitcast.79, bf16[2,16,128,4,64]{2,1,0,4,3:T(8,128)(2,1)} %copy.77, f32[2]{0:T(128)S(1)} %copy-done.13), kind=kLoop, calls=%fused_computation | loop fusion | flops 4194304 | bytes 10485768 | tf_op jit(solution)/shard_map/add | solution.py:390
  144.2 2.4 fusion.38
  146.7 3.1 %copy.68.kern_ref = f32[2,16,128,128]{3,2,1,0:T(8,128)} copy(f32[2,16,128,128]{2,1,0,3:T(8,128)} %bitcast.81) | data formatting | bytes 4194304 | tf_op jit(solution)/shard_map/reshape | solution.py:414
  151.3 13.2 %shard_map.147 = f32[2,4,2,256,128]{4,3,2,1,0:T(8,128)S(1)} custom-call(s32[1]{0:T(128)} %bitcast.mine_ref, f32[4,2,512,128]{3,2,1,0:T(8,128)S(1)} %copy-done.7, f32[2,16,128,128]{3,2,1,0:T(8,128)} %copy.68.kern_ref, f32[2,1,8,128]{3,2,1,0:T(8,128)S(1)} %slice.89.mirror_ref, bf16[2,128,128]{2,1,0:T(8,128)(2,1)S(1)} %copy-done.10, ...), custom_call_target="tpu_custom_call" | custom-call | flops 1610612736 | bytes 16777216 | tf_op jit(solution)/shard_map/pallas_call | solution.py:416
  168.6 3.1 %copy.66.kern_ref = f32[2,16,128,128]{3,2,1,0:T(8,128)} copy(f32[2,16,128,128]{2,1,0,3:T(8,128)} %bitcast.80) | data formatting | bytes 4194304 | tf_op jit(solution)/shard_map/reshape | solution.py:414
  171.7 12.1 %all-to-all-done.in_ref = f32[4,2,512,128]{3,2,1,0:T(8,128)S(1)} async-done(((f32[4,2,512,128]{3,2,1,0:T(8,128)}), f32[4,2,512,128]{3,2,1,0:T(8,128)S(1)}, u32[]{:S(2)}, u32[]{:S(2)}) %all-to-all-start) | async-done | bytes 2097184 | tf_op jit(solution)/shard_map/all_to_all | solution.py:385
  186.6 14.9 %shard_map.146 = f32[2,4,2,256,128]{4,3,2,1,0:T(8,128)S(1)} custom-call(s32[1]{0:T(128)} %bitcast.mine_ref, f32[4,2,512,128]{3,2,1,0:T(8,128)S(1)} %copy-done.3, f32[2,16,128,128]{3,2,1,0:T(8,128)} %copy.66.kern_ref, f32[2,16,128,128]{3,2,1,0:T(8,128)} %copy-done.12, bf16[2,128,128]{2,1,0:T(8,128)(2,1)S(1)} %copy-done.10, ...), custom_call_target="tpu_custom_call" | custom-call | flops 1610612736 | bytes 16777216 | tf_op jit(solution)/shard_map/pallas_call | solution.py:416
  202.7 3.5 %all-to-all-start.3 = ((f32[4,2,256,128]{3,2,1,0:T(8,128)}), f32[4,2,256,128]{3,2,1,0:T(8,128)S(1)}, u32[]{:S(2)}, u32[]{:S(2)}) async-start(f32[4,2,256,128]{3,2,1,0:T(8,128)} %fusion), calls=%async_computation.3 | async-start | bytes 2097152 | tf_op jit(solution)/shard_map/all_to_all | solution.py:432
  207.9 22.6 %collective-permute-done.2 = f32[4,2,256,128]{3,2,1,0:T(8,128)S(1)} collective-permute-done((f32[4,2,256,128]{3,2,1,0:T(8,128)S(1)}, f32[4,2,256,128]{3,2,1,0:T(8,128)S(1)}, u32[]{:S(2)}, u32[]{:S(2)}) %collective-permute-start.2) | collective-permute-done | bytes 1048608 | tf_op jit(solution)/shard_map/ppermute | solution.py:429
  231.5 28.5 %all_to_all.20.refs_0_ = f32[4,2,256,128]{3,2,1,0:T(8,128)S(1)} all-to-all(f32[4,2,256,128]{3,2,1,0:T(8,128)} %fusion.1), channel_id=1, replica_groups=mesh['grp'=2,'pencil'=4,'depth'=2,'mem'=2] {'pencil'}, dimensions={0} | all-to-all | bytes 2097152 | tf_op jit(solution)/shard_map/all_to_all | solution.py:432
  261.7 5.3 %shard_map.148 = f32[1,256,2048]{2,1,0:T(8,128)} custom-call(f32[4,2,256,128]{3,2,1,0:T(8,128)S(1)} %all_to_all.20.refs_0_, f32[4,2,256,128]{3,2,1,0:T(8,128)S(1)} %all-to-all-done.3.refs_1_, bf16[8,512,256]{2,1,0:T(8,128)(2,1)S(1)} %copy-done.11, bf16[8,512,256]{2,1,0:T(8,128)(2,1)} %constant.126.clone.refs_3_), custom_call_target="tpu_custom_call" | custom-call | flops 3221225472 | bytes 8388608 | tf_op jit(solution)/shard_map/pallas_call | solution.py:435
  (72 shorter events, 26.4 us)
Async XLA Ops:
  6.5 40.7 %copy-start = (f32[8,1]{0,1:T(1,128)S(1)}, f32[8,1]{0,1:T(1,128)}, u32[]{:S(2)}) copy-start(f32[8,1]{0,1:T(1,128)} %param.16) | copy-start | bytes 100
  6.5 95.5 %all-gather.2.cloned.1.call-start = ((), (), s32[]{:S(2)}) async-start(), calls=%async_computation.4 | async-start | bytes 5242880 | tf_op jit(solution)/shard_map/all_gather | solution.py:365
  21.5 23.6 %collective-permute-start.1 = (f32[3,4,128,128]{2,3,0,1:T(8,128)S(1)}, f32[3,4,128,128]{2,3,0,1:T(8,128)S(1)}, u32[]{:S(2)}, u32[]{:S(2)}) collective-permute-start(f32[3,4,128,128]{2,3,0,1:T(8,128)S(1)} %rev.2), channel_id=1, source_target_pairs={{0,12},{4,8},{8,4},{12,0},{1,13},{5,9},{9,5},{13,1},{2,14},{6,10},... | collective-permute-start | bytes 2359304 | tf_op jit(solution)/shard_map/ppermute | solution.py:361
  26.6 0.7 collective-permute-start
  56.5 1.3 copy-start.8
  57.8 1.4 copy-start.9
  59.2 71.7 %all-to-all-start.2 = ((f32[4,2,512,128]{3,2,1,0:T(8,128)}), f32[4,2,512,128]{3,2,1,0:T(8,128)S(1)}, u32[]{:S(2)}, u32[]{:S(2)}) async-start(f32[4,2,512,128]{3,2,1,0:T(8,128)} %copy-done.9), calls=%async_computation.2 | async-start | bytes 4194304 | tf_op jit(solution)/shard_map/all_to_all | solution.py:385
  130.9 1.4 copy-start.6
  132.3 3.9 %copy-start.13 = (f32[2]{0:T(128)S(1)}, f32[2]{0:T(128)}, u32[]{:S(2)}) copy-start(f32[2]{0:T(128)} %constant.119.clone) | copy-start | bytes 28
  132.3 51.4 %all-to-all-start = ((f32[4,2,512,128]{3,2,1,0:T(8,128)}), f32[4,2,512,128]{3,2,1,0:T(8,128)S(1)}, u32[]{:S(2)}, u32[]{:S(2)}) async-start(f32[4,2,512,128]{3,2,1,0:T(8,128)} %copy-done.8), calls=%async_computation | async-start | bytes 4194304 | tf_op jit(solution)/shard_map/all_to_all | solution.py:385
  142.3 1.4 copy-start.12
  146.7 3.1 %copy-start.10 = (bf16[2,128,128]{2,1,0:T(8,128)(2,1)S(1)}, bf16[2,128,128]{2,1,0:T(8,128)(2,1)}, u32[]{:S(2)}) copy-start(bf16[2,128,128]{2,1,0:T(8,128)(2,1)} %constant.124.clone.swap_ref) | copy-start | bytes 196612
  149.8 1.6 copy-start.7
  164.6 1.4 copy-start.4
  167.1 34.5 %collective-permute-start.3 = (f32[4,2,256,128]{3,2,1,0:T(8,128)}, f32[4,2,256,128]{3,2,1,0:T(8,128)S(1)}, u32[]{:S(2)}, u32[]{:S(2)}) collective-permute-start(f32[4,2,256,128]{3,2,1,0:T(8,128)} %slice_bitcast_fusion), channel_id=1, source_target_pairs={{0,2},{2,0},{1,3},{3,1},{4,6},{6,4},{5,7},{7,5},{8,10},{10,8},{9,1... | collective-permute-start | bytes 3145736 | tf_op jit(solution)/shard_map/ppermute | solution.py:429
  183.7 1.3 copy-start.2
  185.0 1.6 copy-start.3
  186.6 15.0 %copy-start.5 = (f32[2,4,2,256,128]{4,3,2,1,0:T(8,128)S(1)}, f32[2,4,2,256,128]{4,3,2,1,0:T(8,128)}, u32[]{:S(2)}) copy-start(f32[2,4,2,256,128]{4,3,2,1,0:T(8,128)} %copy-done.4) | copy-start | bytes 6291460
  202.7 28.9 %all-to-all-start.3 = ((f32[4,2,256,128]{3,2,1,0:T(8,128)}), f32[4,2,256,128]{3,2,1,0:T(8,128)S(1)}, u32[]{:S(2)}, u32[]{:S(2)}) async-start(f32[4,2,256,128]{3,2,1,0:T(8,128)} %fusion), calls=%async_computation.3 | async-start | bytes 2097152 | tf_op jit(solution)/shard_map/all_to_all | solution.py:432
  206.3 24.2 %collective-permute-start.2 = (f32[4,2,256,128]{3,2,1,0:T(8,128)S(1)}, f32[4,2,256,128]{3,2,1,0:T(8,128)S(1)}, u32[]{:S(2)}, u32[]{:S(2)}) collective-permute-start(f32[4,2,256,128]{3,2,1,0:T(8,128)S(1)} %slice_bitcast_fusion.2), channel_id=1, source_target_pairs={{0,2},{2,0},{1,3},{3,1},{4,6},{6,4},{5,7},{7,5},{8,10},{10,8},{9,1... | collective-permute-start | bytes 3145736 | tf_op jit(solution)/shard_map/ppermute | solution.py:429
  260.1 1.6 copy-start.11
  261.7 5.3 %copy-start.1 = (f32[8,1]{0,1:T(1,128)S(1)}, f32[8,1]{0,1:T(1,128)}, u32[]{:S(2)}) copy-start(f32[8,1]{0,1:T(1,128)} %param.16) | copy-start | bytes 100
Sparse Core Ops, SparseCore 0:
  46.7 55.2 all-gather.1

commit v2 on v1

--- a/solution.py
+++ b/solution.py
@@ -203,11 +203,27 @@
                     outs[place][pencil, c] = total[:, begin : begin + HALF]
 
 
-def columns_kernel(special, mine_ref, in_ref, kern_ref, mirror_ref, swap_ref, fh_ref, fl_ref, ih_ref, il_ref,
-                   out_ref, pieces, waves):
+def mirror_kernel(where_ref, in_ref, swap_ref, turn_ref, zero_ref, *rest_refs):
+    per = in_ref.shape[2] // INNER
+    swap = swap_ref[jnp.where(where_ref[1] + pl.program_id(0) == 0, 0, 1)]
+    for j in range(per):
+        turn = turn_ref[jnp.where(where_ref[2] == 0, 0, 1) if j == 0 else 1]
+        turned = [dot(in_ref[c, :, j * INNER : (j + 1) * INNER], turn) for c in range(2)]
+        value = dot(swap, jnp.concatenate(turned, axis=1).astype(bf16))
+        if j == 0:
+            zero_ref[0, 0] = value
+        else:
+            rest_refs[0][per - 1 - j, 0] = value
+
+
+def columns_kernel(special, where_ref, in_ref, kern_ref, mirror_ref, edge_ref, swap_ref, pick_ref,
+                   fh_ref, fl_ref, ih_ref, il_ref, out_ref, pieces, waves):
     part_rows = in_ref.shape[2]
-    depths, pencils, _, out_rows, _ = out_ref.shape
-    mine = mine_ref[0]
+    depths, pencils, _, out_rows, lanes = out_ref.shape
+    share = mirror_ref.shape[1]
+    steps = RADIX // share
+    mine = where_ref[0]
+    now = pl.program_id(0)
 
     def forward(b, carry):
         values = []
@@ -222,36 +238,58 @@
             pieces[r, also, :] = im
         return carry
 
-    lax.fori_loop(0, INNER // 8, forward, 0)
-
-    def wave(r):
+    @pl.when(now == 0)
+    def _():
+        lax.fori_loop(0, INNER // 8, forward, 0)
+
+    def wave(r, u):
         high, low = split_value(pieces[r])
-        return dot(fh_ref[r], high) + dot(fh_ref[r], low) + dot(fl_ref[r], high)
-
-    def finish(r, got, extra):
+        return dot(fh_ref[u], high) + dot(fh_ref[u], low) + dot(fl_ref[u], high)
+
+    def finish(r, u, got):
         re, im = got[:INNER], got[INNER:]
-        kr, ki = kern_ref[0, r], kern_ref[1, r]
-        sr, si = re * kr - im * ki, re * ki + im * kr
-        if extra is not None:
-            sr, si = sr + extra[0], si + extra[1]
+        tiles = [mirror_ref[j, u] for j in range(mirror_ref.shape[0])]
+        rows = slice(u * INNER, (u + 1) * INNER)
+        parts = []
+        for c in range(2):
+            other = [tile[:, c * HALF : (c + 1) * HALF] for tile in tiles]
+            other = jnp.concatenate(other, axis=1) if len(other) > 1 else other[0]
+            own = dot(kern_ref[c, rows, :], pick_ref[...])
+            parts.append(own + 0.5 * other if c == 0 else own - 0.5 * other)
+        kr, ki = parts
+        if special:
+            other = lax.rem(RADIX - r, RADIX)
+            high, low = split_value(waves[other])
+            swap = swap_ref[jnp.where(r == 0, 0, 1)]
+            ore = dot(swap, high[:INNER]) + dot(swap, low[:INNER])
+            oim = -(dot(swap, high[INNER:]) + dot(swap, low[INNER:]))
+            mask = (lax.broadcasted_iota(jnp.int32, (INNER, lanes), 1) == 0) & (where_ref[2] == 0)
+            hr = jnp.where(mask, 0.5 * (kr - edge_ref[0, u]), 0.0)
+            hi = jnp.where(mask, 0.5 * (ki - edge_ref[1, u]), 0.0)
+            kr, ki = kr - hr, ki - hi
+            sr = re * kr - im * ki + (ore * hr - oim * hi)
+            si = re * ki + im * kr + (ore * hi + oim * hr)
+        else:
+            sr, si = re * kr - im * ki, re * ki + im * kr
         spectrum = jnp.concatenate([sr, si], axis=0)
         high, low = split_value(spectrum)
-        pieces[r] = dot(ih_ref[r], high) + dot(ih_ref[r], low) + dot(il_ref[r], high)
+        pieces[r] = dot(ih_ref[u], high) + dot(ih_ref[u], low) + dot(il_ref[u], high)
 
     if special:
-        for r in range(RADIX):
-            waves[r] = wave(r)
-        for r in range(RADIX):
-            other = (RADIX - r) % RADIX
-            high, low = split_value(waves[other])
-            swap = swap_ref[0 if r == 0 else 1]
-            re = dot(swap, high[:INNER]) + dot(swap, low[:INNER])
-            im = -(dot(swap, high[INNER:]) + dot(swap, low[INNER:]))
-            kr, ki = mirror_ref[0, r], mirror_ref[1, r]
-            finish(r, waves[r], (re * kr - im * ki, re * ki + im * kr))
+        @pl.when(now < steps)
+        def _():
+            for u in range(share):
+                waves[now * share + u] = wave(now * share + u, u)
+
+        @pl.when(now >= steps)
+        def _():
+            for u in range(share):
+                r = (now - steps) * share + u
+                finish(r, u, waves[r])
     else:
-        for r in range(RADIX):
-            finish(r, wave(r), None)
+        for u in range(share):
+            r = now * share + u
+            finish(r, u, wave(r, u))
 
     def backward(b, carry):
         at = pl.ds(pl.multiple_of(b * 8, 8), 8)
@@ -266,7 +304,9 @@
             out_ref[depth, pencil, 1, put, :] = im
         return carry
 
-    lax.fori_loop(0, INNER // 8, backward, 0)
+    @pl.when(now == pl.num_programs(0) - 1)
+    def _():
+        lax.fori_loop(0, INNER // 8, backward, 0)
 
 
 def fields_kernel(pencils, width, *refs):
@@ -330,39 +370,36 @@
 
     kern_count = kernel_spectra.shape[0]
     local = layer_kernel[0] - lax.axis_index("depth") * kern_count
-    kernel = lax.dynamic_index_in_dim(kernel_spectra, local, 0, keepdims=False)
-    kernel = kernel.reshape(2, RADIX, INNER, per, INNER)
     share = RADIX // sharers
     first = lax.axis_index(("grp", "mem")) * share
-    taken = jnp.stack(
-        [
-            lax.dynamic_index_in_dim(kernel, lax.rem(RADIX - first - i, RADIX), 1, keepdims=False)
-            for i in range(share)
-        ],
-        axis=0,
-    )
-    shape = (share, INNER, INNER)
-    to = lax.broadcasted_iota(jnp.int32, shape, 1)
-    is_zero = (lax.broadcasted_iota(jnp.int32, shape, 0) + first) == 0
-    swap_x = (
-        lax.broadcasted_iota(jnp.int32, shape, 2) == jnp.where(is_zero, (INNER - to) % INNER, INNER - 1 - to)
-    ).astype(bf16)
-    shape = (per, INNER, HALF)
-    to = lax.broadcasted_iota(jnp.int32, shape, 2)
-    is_zero = (lax.broadcasted_iota(jnp.int32, shape, 0) + pencil) == 0
-    swap_y = (
-        lax.broadcasted_iota(jnp.int32, shape, 1) == jnp.where(is_zero, (INNER - to) % INNER, INNER - 1 - to)
-    ).astype(bf16)
-    turned = jnp.einsum("icbjq,jqt->jibct", taken, swap_y, preferred_element_type=bf16)
-    turned = turned.reshape(per, share, INNER, 2 * HALF)
-    turned = jnp.einsum("iab,jibs->jias", swap_x, turned, preferred_element_type=f32)
-    mirrored = lax.ppermute(turned[:1], "pencil", [(p, (pencils - p) % pencils) for p in range(pencils)])
+    index = np.arange(INNER)
+    swaps = np.zeros((2, INNER, INNER), np.float32)
+    swaps[0, index, (INNER - index) % INNER] = 1.0
+    swaps[1, index, INNER - 1 - index] = 1.0
+    turns = jnp.asarray(swaps.transpose(0, 2, 1)[:, :, :HALF].astype(bf16))
+    swaps = jnp.asarray(swaps.astype(bf16))
+    groups = [1] if per == 1 else [1, per - 1]
+    moved = pl.pallas_call(
+        mirror_kernel,
+        grid_spec=pltpu.PrefetchScalarGridSpec(
+            num_scalar_prefetch=1,
+            grid=(share,),
+            in_specs=[
+                pl.BlockSpec(
+                    (None, 2, INNER, per * INNER), lambda i, w: (w[0], 0, lax.rem(RADIX - w[1] - i, RADIX), 0)
+                ),
+                pl.BlockSpec((2, INNER, INNER), lambda i, w: (0, 0, 0)),
+                pl.BlockSpec((2, INNER, HALF), lambda i, w: (0, 0, 0)),
+            ],
+            out_specs=[pl.BlockSpec((g, 1, INNER, INNER), lambda i, w: (0, i, 0, 0)) for g in groups],
+        ),
+        out_shape=[jax.ShapeDtypeStruct((g, share, INNER, INNER), f32) for g in groups],
+        compiler_params=params(),
+        cost_estimate=pl.CostEstimate(flops=1 << 20, bytes_accessed=2 << 20, transcendentals=0),
+    )(jnp.stack([local, first, pencil]), kernel_spectra, swaps, turns)
+    mirrored = lax.ppermute(moved[0], "pencil", [(p, (pencils - p) % pencils) for p in range(pencils)])
     if per > 1:
-        rest = lax.ppermute(
-            turned[:0:-1], "pencil", [(p, pencils - 1 - p) for p in range(pencils)]
-        )
-        mirrored = jnp.concatenate([mirrored, rest], axis=0)
-    mirrored = lax.all_gather(mirrored, ("grp", "mem"), axis=1, tiled=True)
+        rest = lax.ppermute(moved[1], "pencil", [(p, pencils - 1 - p) for p in range(pencils)])
 
     offset = lax.dynamic_index_in_dim(background[:, 0], member_ids[0], 0, keepdims=True)
     row_high, row_low = halves(row_tables())
@@ -383,53 +420,84 @@
         cost_estimate=pl.CostEstimate(flops=6 * part_rows * 2 * LENGTH * 512, bytes_accessed=12 << 20, transcendentals=0),
     )(offset, density, row_high, row_low)
     arrived = [lax.all_to_all(part, "pencil", 0, 0, tiled=True) for part in sent]
-
-    own = kernel[..., :HALF].astype(f32)
+    if per > 1:
+        mirrored = jnp.concatenate([mirrored, rest], axis=0)
+    mirrored, _ = lax.optimization_barrier((mirrored, sent[0]))
+    mirrored = lax.all_gather(mirrored, ("grp", "mem"), axis=0)
+
     sign = jnp.array([0.5, -0.5], f32)
-    mirrored = mirrored.reshape(per, RADIX, INNER, 2, HALF).transpose(3, 1, 2, 0, 4)
-    hermitian = 0.5 * own + sign.reshape(2, 1, 1, 1, 1) * mirrored
-    edge = kernel[:, :, :, 0, HALF].astype(f32)
+    edge = lax.dynamic_slice(kernel_spectra, (local, 0, 0, HALF), (1, 2, LENGTH, 1))
+    edge = edge.reshape(2, RADIX, INNER).astype(f32)
     flipped = jnp.concatenate([edge[:, :1], edge[:, :0:-1]], axis=1)[..., ::-1]
     flipped = jnp.concatenate([jnp.roll(flipped[:, :1], 1, axis=2), flipped[:, 1:]], axis=1)
     edge = 0.5 * edge + sign.reshape(2, 1, 1) * flipped
-    zero = hermitian[..., 0, 0]
-    both = jnp.where(pencil == 0, 0.5 * (zero + edge), zero)
-    apart = jnp.where(pencil == 0, 0.5 * (zero - edge), 0.0)
-    place = lax.broadcasted_iota(jnp.int32, (per, HALF), 0) + lax.broadcasted_iota(jnp.int32, (per, HALF), 1)
-    hermitian = jnp.where(place == 0, both[..., None, None], hermitian)
-    apart = jnp.where(lax.broadcasted_iota(jnp.int32, (lanes,), 0) == 0, apart[..., None], 0.0)
+    edge = jnp.where(lax.broadcasted_iota(jnp.int32, (lanes,), 0) == 0, edge[..., None], 0.0)
 
     column = column_tables()
     tables = halves(column) + halves(column.transpose(0, 2, 1))
-    index = np.arange(INNER)
-    swaps = np.zeros((2, INNER, INNER), np.float32)
-    swaps[0, index, (INNER - index) % INNER] = 1.0
-    swaps[1, index, INNER - 1 - index] = 1.0
-    swaps = jnp.asarray(swaps.astype(bf16))
+    pick = np.zeros((width * INNER, lanes), np.float32)
+    for j in range(width):
+        pick[j * INNER + np.arange(HALF), j * HALF + np.arange(HALF)] = 0.5
+    pick = jnp.asarray(pick.astype(bf16))
     two = depths == 2
     mine = lax.axis_index("depth") if two else jnp.int32(0)
-    mine = mine.reshape(1)
+    where = jnp.stack([mine, local, pencil])
     fields = []
+    before = None
     for k in range(chunks):
-        factors = hermitian[..., k * width : (k + 1) * width, :].reshape(2, RADIX, INNER, lanes)
         special = k == 0
+        steps = sharers
+
+        def early(i, special=special):
+            return jnp.minimum(i, steps - 1) if special else i
+
+        def late(i, special=special):
+            return jnp.maximum(i - steps, 0) if special else i
+
+        here = arrived[k]
+        if before is not None:
+            here, before = lax.optimization_barrier((here, before))
+            fields.append(lax.all_to_all(before, "pencil", 0, 0, tiled=True))
+        edge_block = (2, share, INNER, lanes) if special else (2, 1, 8, lanes)
         out = pl.pallas_call(
             functools.partial(columns_kernel, special),
-            in_specs=[smem] + [vmem] * 8,
-            out_specs=vmem,
+            grid_spec=pltpu.PrefetchScalarGridSpec(
+                num_scalar_prefetch=1,
+                grid=(2 * steps if special else steps,),
+                in_specs=[
+                    pl.BlockSpec((pencils, 2, part_rows, lanes), lambda i, w: (0, 0, 0, 0)),
+                    pl.BlockSpec(
+                        (None, 2, share * INNER, width * INNER), lambda i, w, k=k, late=late: (w[1], 0, late(i), k)
+                    ),
+                    pl.BlockSpec(
+                        (None, width, share, INNER, INNER), lambda i, w, k=k, late=late: (late(i), k, 0, 0, 0)
+                    ),
+                    pl.BlockSpec(
+                        edge_block,
+                        (lambda i, w, late=late: (0, late(i), 0, 0)) if special else (lambda i, w: (0, 0, 0, 0)),
+                    ),
+                    pl.BlockSpec((2, INNER, INNER), lambda i, w: (0, 0, 0)),
+                    pl.BlockSpec(pick.shape, lambda i, w: (0, 0)),
+                ]
+                + [pl.BlockSpec((share, 256, 256), lambda i, w, early=early: (early(i), 0, 0))] * 2
+                + [pl.BlockSpec((share, 256, 256), lambda i, w, late=late: (late(i), 0, 0))] * 2,
+                out_specs=pl.BlockSpec((depths, pencils, 2, out_rows, lanes), lambda i, w: (0, 0, 0, 0, 0)),
+                scratch_shapes=[
+                    pltpu.VMEM((RADIX, 256, lanes), f32),
+                    pltpu.VMEM((RADIX if special else 1, 256, lanes), f32),
+                ],
+            ),
             out_shape=jax.ShapeDtypeStruct((depths, pencils, 2, out_rows, lanes), f32),
-            scratch_shapes=[
-                pltpu.VMEM((RADIX, 256, lanes), f32),
-                pltpu.VMEM((RADIX if special else 1, 256, lanes), f32),
-            ],
             compiler_params=params(),
-            cost_estimate=pl.CostEstimate(flops=12 * RADIX * 256 * 256 * lanes, bytes_accessed=16 << 20, transcendentals=0),
-        )(mine, arrived[k], factors, apart if special else apart[:, :1, :8], swaps, *tables)
+            cost_estimate=pl.CostEstimate(
+                flops=12 * RADIX * 256 * 256 * lanes, bytes_accessed=16 << 20, transcendentals=0
+            ),
+        )(where, here, kernel_spectra, mirrored, edge, swaps, pick, *tables)
         if two:
-            out = out[0] + lax.ppermute(out[1], "depth", [(0, 1), (1, 0)])
+            before = out[0] + lax.ppermute(out[1], "depth", [(0, 1), (1, 0)])
         else:
-            out = lax.psum_scatter(out, "depth", scatter_dimension=0, tiled=False)
-        fields.append(lax.all_to_all(out, "pencil", 0, 0, tiled=True))
+            before = lax.psum_scatter(out, "depth", scatter_dimension=0, tiled=False)
+    fields.append(lax.all_to_all(before, "pencil", 0, 0, tiled=True))
 
     back_high, back_low = halves(inverse_row_tables())
     return pl.pallas_call(

time: 275 us -> 246 us (0.89)
  blocking collectives: 28.5 us -> 99.4 us
  local copies, waits for them, and re-layouts: 57.8 us -> 5.71 us
  waiting for transfers between devices: 79.6 us -> 51.3 us
  starting transfers between devices: 40.7 us -> 16.8 us
  Pallas kernels: 42.2 us -> 48.7 us
    all_to_all x1 -> x2, blocking collectives: 28.5 us -> 99.4 us  [the longest x1 71.6 us: body(): lax.all_to_all(part, 'pencil', 0, 0, tiled=True)]
    all_to_all x2 -> x1, waiting for transfers between devices: 35.6 us -> 0.57 us  [body(): lax.all_to_all(part, 'pencil', 0, 0, tiled=True)]
    all_to_all x2 -> x1, starting transfers between devices: 28.3 us -> 3.74 us  [body(): lax.all_to_all(part, 'pencil', 0, 0, tiled=True)]
    unnamed x30 -> x19, local copies, waits for them, and re-layouts: 21.4 us -> 4.65 us
    reshape x3 -> x0, local copies, waits for them, and re-layouts: 13.1 us -> none  [the longest x1 6.95 us: body(): kernel = kernel.reshape(2, RADIX, INNER, per, INNER)]
    ppermute x4, waiting for transfers between devices: 40.4 us -> 50.7 us  [the longest x2 44.2 us: body(): before = out[0] + lax.ppermute(out[1], 'depth', [(0, 1), (1, 0)])]
    slice x5 -> x0, local copies, waits for them, and re-layouts: 8.4 us -> none  [the longest x1 5.91 us: body(): edge = kernel[:, :, :, 0, HALF].astype(f32)]
    pallas_call x2 -> x3, Pallas kernels: 28.2 us -> 34.6 us  [the longest x2 28.9 us: body(): pl.pallas_call(functools.partial(columns_kernel, special), grid_spec=pltp...]
  transfers between devices with their start and end apart: 8 -> 7, of which waited for: 5 -> 4; matrix products, arithmetic and copies ran while one was open for 14% -> 3% of each run, Pallas kernels for 13% -> 15%
where the time goes in v2:
time: 246 us; the launch traced here: 245 us
  blocking collectives  99.4 us (40%)
  waiting for transfers between devices  51.3 us (21%)
  Pallas kernels  48.7 us (20%)
  starting transfers between devices  16.8 us (7%)
  between operations  14.9 us (6%)
  other arithmetic  8.64 us (4%)
  local copies, waits for them, and re-layouts  5.71 us (2%)
    all_to_all x1, blocking collectives, body(): lax.all_to_all(part, 'pencil', 0, 0, tiled=True)  71.6 us
    ppermute x2, waiting for transfers between devices, body(): before = out[0] + lax.ppermute(out[1], 'depth', [(0, 1), (1, 0)])  44.2 us
    pallas_call x2, Pallas kernels, body(): pl.pallas_call(functools.partial(columns_kernel, special), grid_spec=pltp...  28.9 us
    all_to_all x1, blocking collectives, body(): fields.append(lax.all_to_all(before, 'pencil', 0, 0, tiled=True))  27.8 us
    pallas_call x1, Pallas kernels, body(): pl.pallas_call(functools.partial(rows_kernel, pencils, width), grid=(part...  8.68 us
    ppermute x1, waiting for transfers between devices, body(): lax.ppermute(moved[1], 'pencil', [(p, pencils - 1 - p) for p in range(pen...  6.54 us
    pallas_call x1, Pallas kernels, body(): pl.pallas_call(mirror_kernel, grid_spec=pltpu.PrefetchScalarGridSpec(num_...  5.75 us
    pallas_call x1, Pallas kernels, body(): pl.pallas_call(functools.partial(fields_kernel, pencils, width), in_specs...  5.35 us
  transfers between devices with their start and end apart: 7, of which 4 were waited for; matrix products, arithmetic and copies ran while one was open for 3% of the time, Pallas kernels for 15%

profile of v2, /device:TPU:0, one launch (start us, length us, event | category | flops | bytes accessed | tf_op | source)
XLA Modules:
  0.0 245.4 jit_solution(6147946757664609378)
XLA Ops:
  7.3 0.8 copy-done.3
  8.1 0.8 copy-done.6
  9.0 5.8 %shard_map.164 = (f32[1,4,128,128]{3,2,1,0:T(8,128)S(1)}, f32[3,4,128,128]{3,2,1,0:T(8,128)S(1)}) custom-call(s32[3]{0:T(128)S(1)} %add_add_fusion.1.where_ref, bf16[2,2,2048,512]{3,2,1,0:T(8,128)(2,1)} %kern_ref.3, bf16[2,128,128]{2,1,0:T(8,128)(2,1)S(1)} %copy-done.3, bf16[2,128,64]{2,1,0:T(8,128)(2,1)S(1)} %copy-done.6), custom_call_target="tpu_custom_call" | custom-call | flops 1048576 | bytes 2097152 | tf_op jit(solution)/shard_map/pallas_call | solution.py:382
  14.7 5.1 %collective-permute-start.1 = (f32[3,4,128,128]{3,2,1,0:T(8,128)S(1)}, f32[3,4,128,128]{3,2,1,0:T(8,128)}, u32[]{:S(2)}, u32[]{:S(2)}) collective-permute-start(f32[3,4,128,128]{3,2,1,0:T(8,128)S(1)} %get-tuple-element.15), channel_id=1, source_target_pairs={{0,12},{4,8},{8,4},{12,0},{1,13},{5,9},{9,5},{13,1},{2,14},{6,10},... | collective-permute-start | bytes 2359304 | tf_op jit(solution)/shard_map/ppermute | solution.py:402
  21.8 8.7 %shard_map.163 = (f32[4,2,512,128]{3,2,1,0:T(8,128)S(1)}, f32[4,2,512,128]{3,2,1,0:T(8,128)S(1)}) custom-call(f32[1]{0:T(128)} %bitcast.1.offset_ref, f32[1,1,512,2048]{3,2,1,0:T(8,128)} %in_ref.2, bf16[8,512,256]{2,1,0:T(8,128)(2,1)} %constant.60.clone.high_ref, bf16[8,512,256]{2,1,0:T(8,128)(2,1)} %constant.61.clone.low_ref), custom_call_target="tpu_custom_call" | custom-call | flops 6442450944 | bytes 12582912 | tf_op jit(solution)/shard_map/pallas_call | solution.py:407
  30.5 1.3 copy-done.2
  31.9 6.5 %collective-permute-done.1 = f32[3,4,128,128]{3,2,1,0:T(8,128)} collective-permute-done((f32[3,4,128,128]{3,2,1,0:T(8,128)S(1)}, f32[3,4,128,128]{3,2,1,0:T(8,128)}, u32[]{:S(2)}, u32[]{:S(2)}) %collective-permute-start.1) | collective-permute-done | bytes 786464 | tf_op jit(solution)/shard_map/ppermute | solution.py:402
  38.4 2.3 pad_maximum_fusion
  40.8 71.6 %all_to_all.20.in_ref = f32[4,2,512,128]{3,2,1,0:T(8,128)} all-to-all(f32[4,2,512,128]{3,2,1,0:T(8,128)S(1)} %get-tuple-element.13), channel_id=1, replica_groups=mesh['grp'=2,'pencil'=4,'depth'=2,'mem'=2] {'pencil'}, dimensions={0} | all-to-all | bytes 4194304 | tf_op jit(solution)/shard_map/all_to_all | solution.py:422
  112.3 3.7 %all-to-all-start = ((f32[4,2,512,128]{3,2,1,0:T(8,128)}), f32[4,2,512,128]{3,2,1,0:T(8,128)S(1)}, u32[]{:S(2)}, u32[]{:S(2)}) async-start(f32[4,2,512,128]{3,2,1,0:T(8,128)} %copy-done.2), calls=%async_computation | async-start | bytes 4194304 | tf_op jit(solution)/shard_map/all_to_all | solution.py:422
  116.1 2.0 convert_reduce_fusion
  118.6 1.9 broadcast_select_fusion.edge_ref
  120.5 1.6 copy-done.1
  122.1 15.7 %shard_map.165 = f32[2,4,2,256,128]{4,3,2,1,0:T(8,128)S(1)} custom-call(s32[3]{0:T(128)S(1)} %add_add_fusion.where_ref, f32[4,2,512,128]{3,2,1,0:T(8,128)S(1)} %copy-done.1, bf16[2,2,2048,512]{3,2,1,0:T(8,128)(2,1)} %kern_ref.3, f32[4,4,4,128,128]{4,3,2,1,0:T(8,128)} %bitcast.30, f32[2,16,128,128]{3,2,1,0:T(8,128)} %broadcast_select_fusion.edge_ref, ...), custom_call_target="tpu_custom_call" | custom-call | flops 1610612736 | bytes 16777216 | tf_op jit(solution)/shard_map/pallas_call | solution.py:462
  137.9 1.6 collective-permute-start.2
  139.5 22.2 %collective-permute-done.2 = f32[4,2,256,128]{3,2,1,0:T(8,128)S(1)} collective-permute-done((f32[4,2,256,128]{3,2,1,0:T(8,128)S(1)}, f32[4,2,256,128]{3,2,1,0:T(8,128)S(1)}, u32[]{:S(2)}, u32[]{:S(2)}) %collective-permute-start.2) | collective-permute-done | bytes 1048608 | tf_op jit(solution)/shard_map/ppermute | solution.py:497
  161.6 1.1 fusion.1
  163.3 4.2 %all-to-all-start.2 = ((f32[4,2,256,128]{3,2,1,0:T(8,128)}), f32[4,2,256,128]{3,2,1,0:T(8,128)S(1)}, u32[]{:S(2)}, u32[]{:S(2)}) async-start(f32[4,2,256,128]{3,2,1,0:T(8,128)} %fusion.1), calls=%async_computation.2 | async-start | bytes 2097152 | tf_op jit(solution)/shard_map/all_to_all | solution.py:460
  167.5 13.2 %shard_map.166 = f32[2,4,2,256,128]{4,3,2,1,0:T(8,128)S(1)} custom-call(s32[3]{0:T(128)S(1)} %add_add_fusion.where_ref, f32[4,2,512,128]{3,2,1,0:T(8,128)S(1)} %all-to-all-done.in_ref, bf16[2,2,2048,512]{3,2,1,0:T(8,128)(2,1)} %kern_ref.3, f32[4,4,4,128,128]{4,3,2,1,0:T(8,128)} %bitcast.31, f32[2,16,128,128]{3,2,1,0:T(8,128)} %broadcast_select_fusion.edge_ref, ...), custom_call_target="tpu_custom_call" | custom-call | flops 1610612736 | bytes 16777216 | tf_op jit(solution)/shard_map/pallas_call | solution.py:462
  180.7 1.6 collective-permute-start.3
  182.3 22.0 %collective-permute-done.3 = f32[4,2,256,128]{3,2,1,0:T(8,128)S(1)} collective-permute-done((f32[4,2,256,128]{3,2,1,0:T(8,128)S(1)}, f32[4,2,256,128]{3,2,1,0:T(8,128)S(1)}, u32[]{:S(2)}, u32[]{:S(2)}) %collective-permute-start.3) | collective-permute-done | bytes 1048608 | tf_op jit(solution)/shard_map/ppermute | solution.py:497
  204.3 1.1 fusion
  205.3 27.8 %all_to_all.21.refs_1_ = f32[4,2,256,128]{3,2,1,0:T(8,128)S(1)} all-to-all(f32[4,2,256,128]{3,2,1,0:T(8,128)} %fusion), channel_id=1, replica_groups=mesh['grp'=2,'pencil'=4,'depth'=2,'mem'=2] {'pencil'}, dimensions={0} | all-to-all | bytes 2097152 | tf_op jit(solution)/shard_map/all_to_all | solution.py:500
  233.2 5.3 %shard_map.167 = f32[1,256,2048]{2,1,0:T(8,128)} custom-call(f32[4,2,256,128]{3,2,1,0:T(8,128)S(1)} %all-to-all-done.2.refs_0_, f32[4,2,256,128]{3,2,1,0:T(8,128)S(1)} %all_to_all.21.refs_1_, bf16[8,512,256]{2,1,0:T(8,128)(2,1)S(1)} %copy-done.7, bf16[8,512,256]{2,1,0:T(8,128)(2,1)} %constant.69.clone.refs_3_), custom_call_target="tpu_custom_call" | custom-call | flops 3221225472 | bytes 8388608 | tf_op jit(solution)/shard_map/pallas_call | solution.py:503
  (34 shorter events, 2.6 us)
Async XLA Ops:
  6.5 14.6 %copy-start = (f32[8,1]{0,1:T(1,128)S(1)}, f32[8,1]{0,1:T(1,128)}, u32[]{:S(2)}) copy-start(f32[8,1]{0,1:T(1,128)} %param.18) | copy-start | bytes 100
  6.5 114.0 %all-gather.3.cloned.1.call-start = ((), (), s32[]{:S(2)}) async-start(), calls=%async_computation.4 | async-start | bytes 5242880 | tf_op jit(solution)/shard_map/all_gather | solution.py:426
  7.3 0.8 copy-start.3
  8.1 0.8 copy-start.6
  14.7 23.7 %collective-permute-start.1 = (f32[3,4,128,128]{3,2,1,0:T(8,128)S(1)}, f32[3,4,128,128]{3,2,1,0:T(8,128)}, u32[]{:S(2)}, u32[]{:S(2)}) collective-permute-start(f32[3,4,128,128]{3,2,1,0:T(8,128)S(1)} %get-tuple-element.15), channel_id=1, source_target_pairs={{0,12},{4,8},{8,4},{12,0},{1,13},{5,9},{9,5},{13,1},{2,14},{6,10},... | collective-permute-start | bytes 2359304 | tf_op jit(solution)/shard_map/ppermute | solution.py:402
  19.8 12.0 %collective-permute-start = (f32[1,4,128,128]{3,2,1,0:T(8,128)S(1)}, f32[1,4,128,128]{3,2,1,0:T(8,128)S(1)}, u32[]{:S(2)}, u32[]{:S(2)}) collective-permute-start(f32[1,4,128,128]{3,2,1,0:T(8,128)S(1)} %get-tuple-element.14), channel_id=1, source_target_pairs={{0,0},{4,12},{8,8},{12,4},{1,1},{5,13},{9,9},{13,5},{2,2},{6,14},{... | collective-permute-start | bytes 786440 | tf_op jit(solution)/shard_map/ppermute | solution.py:400
  30.5 1.4 copy-start.2
  112.3 6.1 %copy-start.8 = (f32[2]{0:T(128)S(1)}, f32[2]{0:T(128)}, u32[]{:S(2)}) copy-start(f32[2]{0:T(128)} %constant.62.clone) | copy-start | bytes 28
  112.3 51.0 %all-to-all-start = ((f32[4,2,512,128]{3,2,1,0:T(8,128)}), f32[4,2,512,128]{3,2,1,0:T(8,128)S(1)}, u32[]{:S(2)}, u32[]{:S(2)}) async-start(f32[4,2,512,128]{3,2,1,0:T(8,128)} %copy-done.2), calls=%async_computation | async-start | bytes 4194304 | tf_op jit(solution)/shard_map/all_to_all | solution.py:422
  116.1 4.4 %copy-start.4 = (bf16[2,128,128]{2,1,0:T(8,128)(2,1)S(1)}, bf16[2,128,128]{2,1,0:T(8,128)(2,1)}, u32[]{:S(2)}) copy-start(bf16[2,128,128]{2,1,0:T(8,128)(2,1)} %constant.59.clone.swap_ref) | copy-start | bytes 196612
  116.1 4.4 %copy-start.5 = (bf16[256,128]{1,0:T(8,128)(2,1)S(1)}, bf16[256,128]{1,0:T(8,128)(2,1)}, u32[]{:S(2)}) copy-start(bf16[256,128]{1,0:T(8,128)(2,1)} %constant.67.clone.pick_ref) | copy-start | bytes 196612
  120.5 1.6 copy-start.1
  137.9 23.8 %collective-permute-start.2 = (f32[4,2,256,128]{3,2,1,0:T(8,128)S(1)}, f32[4,2,256,128]{3,2,1,0:T(8,128)S(1)}, u32[]{:S(2)}, u32[]{:S(2)}) collective-permute-start(f32[4,2,256,128]{3,2,1,0:T(8,128)S(1)} %slice_bitcast_fusion.2), channel_id=1, source_target_pairs={{0,2},{2,0},{1,3},{3,1},{4,6},{6,4},{5,7},{7,5},{8,10},{10,8},{9,1... | collective-permute-start | bytes 3145736 | tf_op jit(solution)/shard_map/ppermute | solution.py:497
  163.3 42.0 %all-to-all-start.2 = ((f32[4,2,256,128]{3,2,1,0:T(8,128)}), f32[4,2,256,128]{3,2,1,0:T(8,128)S(1)}, u32[]{:S(2)}, u32[]{:S(2)}) async-start(f32[4,2,256,128]{3,2,1,0:T(8,128)} %fusion.1), calls=%async_computation.2 | async-start | bytes 2097152 | tf_op jit(solution)/shard_map/all_to_all | solution.py:460
  180.7 52.5 %copy-start.7 = (bf16[8,512,256]{2,1,0:T(8,128)(2,1)S(1)}, bf16[8,512,256]{2,1,0:T(8,128)(2,1)}, u32[]{:S(2)}) copy-start(bf16[8,512,256]{2,1,0:T(8,128)(2,1)} %constant.68.clone.refs_2_) | copy-start | bytes 6291460
  180.7 23.5 %collective-permute-start.3 = (f32[4,2,256,128]{3,2,1,0:T(8,128)S(1)}, f32[4,2,256,128]{3,2,1,0:T(8,128)S(1)}, u32[]{:S(2)}, u32[]{:S(2)}) collective-permute-start(f32[4,2,256,128]{3,2,1,0:T(8,128)S(1)} %slice_bitcast_fusion), channel_id=1, source_target_pairs={{0,2},{2,0},{1,3},{3,1},{4,6},{6,4},{5,7},{7,5},{8,10},{10,8},{9,1... | collective-permute-start | bytes 3145736 | tf_op jit(solution)/shard_map/ppermute | solution.py:497
Sparse Core Ops, SparseCore 0:
  40.9 55.1 all-gather.2

commit v3 on v2

--- a/solution.py
+++ b/solution.py
@@ -77,11 +77,13 @@
 def column_tables():
     q = np.arange(INNER)[:, None]
     m = np.arange(INNER)[None, :]
-    tables = np.zeros((RADIX, 256, 256))
-    for r in range(RADIX):
-        turn = np.exp(-2j * np.pi * (((RADIX * q + r) * m) % LENGTH) / LENGTH)
-        tables[r] = np.block([[turn.real, -turn.imag], [turn.imag, turn.real]])
-    return tables
+    turn = np.exp(-2j * np.pi * ((q * m) % INNER) / INNER)
+    table = np.block([[turn.real, -turn.imag], [turn.imag, turn.real]])
+    angles = 2 * np.pi * np.arange(RADIX)[:, None] * np.arange(INNER)[None, :] / LENGTH
+    turns = np.zeros((RADIX, INNER, INNER), np.float32)
+    turns[..., 0] = np.cos(angles)
+    turns[..., 1] = np.sin(angles)
+    return table, turns
 
 
 def split_value(value):
@@ -203,11 +205,19 @@
                     outs[place][pencil, c] = total[:, begin : begin + HALF]
 
 
-def mirror_kernel(where_ref, in_ref, swap_ref, turn_ref, zero_ref, *rest_refs):
+def mirror_kernel(where_ref, in_ref, zero_ref, *rest_refs):
     per = in_ref.shape[2] // INNER
-    swap = swap_ref[jnp.where(where_ref[1] + pl.program_id(0) == 0, 0, 1)]
+
+    def swapped(zero, shape, axis):
+        to = lax.broadcasted_iota(jnp.int32, shape, axis)
+        begin = lax.broadcasted_iota(jnp.int32, shape, 1 - axis)
+        total = jnp.where(zero, INNER, INNER - 1)
+        return jnp.where((to + begin == total) | (zero & (to + begin == 0)), 1.0, 0.0).astype(bf16)
+
+    swap = swapped(where_ref[1] + pl.program_id(0) == 0, (INNER, INNER), 0)
+    plain = swapped(where_ref[1] < 0, (INNER, HALF), 1)
     for j in range(per):
-        turn = turn_ref[jnp.where(where_ref[2] == 0, 0, 1) if j == 0 else 1]
+        turn = swapped(where_ref[2] == 0, (INNER, HALF), 1) if j == 0 else plain
         turned = [dot(in_ref[c, :, j * INNER : (j + 1) * INNER], turn) for c in range(2)]
         value = dot(swap, jnp.concatenate(turned, axis=1).astype(bf16))
         if j == 0:
@@ -217,9 +227,10 @@
 
 
 def columns_kernel(special, where_ref, in_ref, kern_ref, mirror_ref, edge_ref, swap_ref, pick_ref,
-                   fh_ref, fl_ref, ih_ref, il_ref, out_ref, pieces, waves):
+                   turns_ref, late_ref, fh_ref, fl_ref, ih_ref, il_ref, out_ref, pieces, waves):
     part_rows = in_ref.shape[2]
-    depths, pencils, _, out_rows, lanes = out_ref.shape
+    depths, splits, pencils, _, split_rows, lanes = out_ref.shape
+    out_rows = splits * split_rows
     share = mirror_ref.shape[1]
     steps = RADIX // share
     mine = where_ref[0]
@@ -243,8 +254,10 @@
         lax.fori_loop(0, INNER // 8, forward, 0)
 
     def wave(r, u):
-        high, low = split_value(pieces[r])
-        return dot(fh_ref[u], high) + dot(fh_ref[u], low) + dot(fl_ref[u], high)
+        re, im = pieces[r, :INNER], pieces[r, INNER:]
+        c, s = turns_ref[u, :, 0:1], turns_ref[u, :, 1:2]
+        high, low = split_value(jnp.concatenate([re * c + im * s, im * c - re * s], axis=0))
+        return dot(fh_ref[...], high) + dot(fh_ref[...], low) + dot(fl_ref[...], high)
 
     def finish(r, u, got):
         re, im = got[:INNER], got[INNER:]
@@ -273,7 +286,11 @@
             sr, si = re * kr - im * ki, re * ki + im * kr
         spectrum = jnp.concatenate([sr, si], axis=0)
         high, low = split_value(spectrum)
-        pieces[r] = dot(ih_ref[u], high) + dot(ih_ref[u], low) + dot(il_ref[u], high)
+        got = dot(ih_ref[...], high) + dot(ih_ref[...], low) + dot(il_ref[...], high)
+        re, im = got[:INNER], got[INNER:]
+        c, s = late_ref[u, :, 0:1], late_ref[u, :, 1:2]
+        pieces[r, :INNER] = re * c - im * s
+        pieces[r, INNER:] = im * c + re * s
 
     if special:
         @pl.when(now < steps)
@@ -299,9 +316,10 @@
             x = n * INNER + b * 8
             pencil = x // (out_rows * depths)
             depth = lax.rem(x // out_rows - mine + depths, depths)
-            put = pl.ds(pl.multiple_of(lax.rem(x, out_rows), 8), 8)
-            out_ref[depth, pencil, 0, put, :] = re
-            out_ref[depth, pencil, 1, put, :] = im
+            part = lax.rem(x, out_rows) // split_rows
+            put = pl.ds(pl.multiple_of(lax.rem(x, split_rows), 8), 8)
+            out_ref[depth, part, pencil, 0, put, :] = re
+            out_ref[depth, part, pencil, 1, put, :] = im
         return carry
 
     @pl.when(now == pl.num_programs(0) - 1)
@@ -309,22 +327,28 @@
         lax.fori_loop(0, INNER // 8, backward, 0)
 
 
-def fields_kernel(pencils, width, *refs):
-    chunks = RADIX // pencils // width
-    ins, (high_ref, low_ref, out_ref, pieces) = refs[:chunks], refs[chunks:]
+def fields_kernel(pencils, width, counts, *refs):
+    ins, at = [], 0
+    for count in counts:
+        ins.append(refs[at : at + count])
+        at += count
+    high_ref, low_ref, out_ref, pieces = refs[at:]
     per = RADIX // pencils
     rows = out_ref.shape[1]
+
+    def read(chunk, pencil, c):
+        found = [ref[pencil, c] for ref in ins[chunk]]
+        return jnp.concatenate(found, axis=0) if len(found) > 1 else found[0]
 
     def pair(t):
         if width == 2:
             pencil, place = divmod(2 * t, per)
-            ref = ins[place // 2]
-            return jnp.concatenate([ref[pencil, 0], ref[pencil, 1]], axis=1)
+            return jnp.concatenate([read(place // 2, pencil, c) for c in range(2)], axis=1)
         found = []
         for c in range(2):
             for odd in range(2):
                 pencil, place = divmod(2 * t + odd, per)
-                found.append(ins[place][pencil, c])
+                found.append(read(place, pencil, c))
         return jnp.concatenate(found, axis=1)
 
     for s in range(8):
@@ -376,7 +400,6 @@
     swaps = np.zeros((2, INNER, INNER), np.float32)
     swaps[0, index, (INNER - index) % INNER] = 1.0
     swaps[1, index, INNER - 1 - index] = 1.0
-    turns = jnp.asarray(swaps.transpose(0, 2, 1)[:, :, :HALF].astype(bf16))
     swaps = jnp.asarray(swaps.astype(bf16))
     groups = [1] if per == 1 else [1, per - 1]
     moved = pl.pallas_call(
@@ -388,15 +411,13 @@
                 pl.BlockSpec(
                     (None, 2, INNER, per * INNER), lambda i, w: (w[0], 0, lax.rem(RADIX - w[1] - i, RADIX), 0)
                 ),
-                pl.BlockSpec((2, INNER, INNER), lambda i, w: (0, 0, 0)),
-                pl.BlockSpec((2, INNER, HALF), lambda i, w: (0, 0, 0)),
             ],
             out_specs=[pl.BlockSpec((g, 1, INNER, INNER), lambda i, w: (0, i, 0, 0)) for g in groups],
         ),
         out_shape=[jax.ShapeDtypeStruct((g, share, INNER, INNER), f32) for g in groups],
         compiler_params=params(),
         cost_estimate=pl.CostEstimate(flops=1 << 20, bytes_accessed=2 << 20, transcendentals=0),
-    )(jnp.stack([local, first, pencil]), kernel_spectra, swaps, turns)
+    )(jnp.stack([local, first, pencil]), kernel_spectra)
     mirrored = lax.ppermute(moved[0], "pencil", [(p, (pencils - p) % pencils) for p in range(pencils)])
     if per > 1:
         rest = lax.ppermute(moved[1], "pencil", [(p, pencils - 1 - p) for p in range(pencils)])
@@ -420,10 +441,6 @@
         cost_estimate=pl.CostEstimate(flops=6 * part_rows * 2 * LENGTH * 512, bytes_accessed=12 << 20, transcendentals=0),
     )(offset, density, row_high, row_low)
     arrived = [lax.all_to_all(part, "pencil", 0, 0, tiled=True) for part in sent]
-    if per > 1:
-        mirrored = jnp.concatenate([mirrored, rest], axis=0)
-    mirrored, _ = lax.optimization_barrier((mirrored, sent[0]))
-    mirrored = lax.all_gather(mirrored, ("grp", "mem"), axis=0)
 
     sign = jnp.array([0.5, -0.5], f32)
     edge = lax.dynamic_slice(kernel_spectra, (local, 0, 0, HALF), (1, 2, LENGTH, 1))
@@ -433,8 +450,14 @@
     edge = 0.5 * edge + sign.reshape(2, 1, 1) * flipped
     edge = jnp.where(lax.broadcasted_iota(jnp.int32, (lanes,), 0) == 0, edge[..., None], 0.0)
 
-    column = column_tables()
-    tables = halves(column) + halves(column.transpose(0, 2, 1))
+    if per > 1:
+        mirrored = jnp.concatenate([mirrored, rest], axis=0)
+    mirrored, edge, _ = lax.optimization_barrier((mirrored, edge, sent[0]))
+    mirrored = lax.all_gather(mirrored, ("grp", "mem"), axis=0)
+
+    column, column_turns = column_tables()
+    column_turns = jnp.asarray(column_turns)
+    tables = halves(column) + halves(column.T)
     pick = np.zeros((width * INNER, lanes), np.float32)
     for j in range(width):
         pick[j * INNER + np.arange(HALF), j * HALF + np.arange(HALF)] = 0.5
@@ -442,7 +465,7 @@
     two = depths == 2
     mine = lax.axis_index("depth") if two else jnp.int32(0)
     where = jnp.stack([mine, local, pencil])
-    fields = []
+    fields, counts = [], []
     before = None
     for k in range(chunks):
         special = k == 0
@@ -455,6 +478,9 @@
             return jnp.maximum(i - steps, 0) if special else i
 
         here = arrived[k]
+        splits = 2 if two and k == chunks - 1 else 1
+        counts.append(splits)
+        split_rows = out_rows // splits
         if before is not None:
             here, before = lax.optimization_barrier((here, before))
             fields.append(lax.all_to_all(before, "pencil", 0, 0, tiled=True))
@@ -479,30 +505,37 @@
                     pl.BlockSpec((2, INNER, INNER), lambda i, w: (0, 0, 0)),
                     pl.BlockSpec(pick.shape, lambda i, w: (0, 0)),
                 ]
-                + [pl.BlockSpec((share, 256, 256), lambda i, w, early=early: (early(i), 0, 0))] * 2
-                + [pl.BlockSpec((share, 256, 256), lambda i, w, late=late: (late(i), 0, 0))] * 2,
-                out_specs=pl.BlockSpec((depths, pencils, 2, out_rows, lanes), lambda i, w: (0, 0, 0, 0, 0)),
+                + [pl.BlockSpec((share, INNER, INNER), lambda i, w, early=early: (early(i), 0, 0))]
+                + [pl.BlockSpec((share, INNER, INNER), lambda i, w, late=late: (late(i), 0, 0))]
+                + [pl.BlockSpec((256, 256), lambda i, w: (0, 0))] * 4,
+                out_specs=pl.BlockSpec(
+                    (depths, splits, pencils, 2, split_rows, lanes), lambda i, w: (0, 0, 0, 0, 0, 0)
+                ),
                 scratch_shapes=[
                     pltpu.VMEM((RADIX, 256, lanes), f32),
                     pltpu.VMEM((RADIX if special else 1, 256, lanes), f32),
                 ],
             ),
-            out_shape=jax.ShapeDtypeStruct((depths, pencils, 2, out_rows, lanes), f32),
+            out_shape=jax.ShapeDtypeStruct((depths, splits, pencils, 2, split_rows, lanes), f32),
             compiler_params=params(),
             cost_estimate=pl.CostEstimate(
                 flops=12 * RADIX * 256 * 256 * lanes, bytes_accessed=16 << 20, transcendentals=0
             ),
-        )(where, here, kernel_spectra, mirrored, edge, swaps, pick, *tables)
-        if two:
-            before = out[0] + lax.ppermute(out[1], "depth", [(0, 1), (1, 0)])
-        else:
-            before = lax.psum_scatter(out, "depth", scatter_dimension=0, tiled=False)
+        )(where, here, kernel_spectra, mirrored, edge, swaps, pick, column_turns, column_turns, *tables)
+        if not two:
+            before = lax.psum_scatter(out[:, 0], "depth", scatter_dimension=0, tiled=False)
+            continue
+        before = out[0, 0] + lax.ppermute(out[1, 0], "depth", [(0, 1), (1, 0)])
+        if splits == 2:
+            second, before = lax.optimization_barrier((out[1, 1], before))
+            fields.append(lax.all_to_all(before, "pencil", 0, 0, tiled=True))
+            before = out[0, 1] + lax.ppermute(second, "depth", [(0, 1), (1, 0)])
     fields.append(lax.all_to_all(before, "pencil", 0, 0, tiled=True))
 
     back_high, back_low = halves(inverse_row_tables())
     return pl.pallas_call(
-        functools.partial(fields_kernel, pencils, width),
-        in_specs=[vmem] * (chunks + 2),
+        functools.partial(fields_kernel, pencils, width, counts),
+        in_specs=[vmem] * (len(fields) + 2),
         out_specs=vmem,
         out_shape=jax.ShapeDtypeStruct((1, out_rows, LENGTH), f32),
         scratch_shapes=[pltpu.VMEM((8, out_rows, 256), f32)],

time: 246 us -> 273 us (1.11)
  local copies, waits for them, and re-layouts: 5.71 us -> 15.5 us
  waiting for transfers between devices: 51.3 us -> 60.2 us
  blocking collectives: 99.4 us -> 105 us
    all_to_all x1, waiting for transfers between devices: 0.01 us -> 11.2 us  [body(): fields.append(lax.all_to_all(before, 'pencil', 0, 0, tiled=True))]
    unnamed x19 -> x37, local copies, waits for them, and re-layouts: 4.65 us -> 13.7 us
    all_to_all x1 -> x2, blocking collectives: 27.8 us -> 33.6 us  [body(): fields.append(lax.all_to_all(before, 'pencil', 0, 0, tiled=True))]
    ppermute x1, waiting for transfers between devices: 6.54 us -> 2.33 us  [body(): lax.ppermute(moved[1], 'pencil', [(p, pencils - 1 - p) for p in range(pen...]
    ppermute x2 -> x3, waiting for transfers between devices: 44.2 us -> 44.6 us  [the longest x2 33.6 us: body(): before = out[0, 0] + lax.ppermute(out[1, 0], 'depth', [(0, 1), (1, 0)])]
  transfers between devices with their start and end apart: 7 -> 8, of which waited for: 4 -> 6; matrix products, arithmetic and copies ran while one was open for 3% -> 3% of each run, Pallas kernels for 15% -> 9%
where the time goes in v3:
time: 273 us; the launch traced here: 272 us
  blocking collectives  105 us (38%)
  waiting for transfers between devices  60.2 us (22%)
  Pallas kernels  50.1 us (18%)
  starting transfers between devices  17.6 us (6%)
  local copies, waits for them, and re-layouts  15.5 us (6%)
  between operations  14.9 us (5%)
  other arithmetic  8.45 us (3%)
    all_to_all x1, blocking collectives, body(): lax.all_to_all(part, 'pencil', 0, 0, tiled=True)  71.6 us
    ppermute x2, waiting for transfers between devices, body(): before = out[0, 0] + lax.ppermute(out[1, 0], 'depth', [(0, 1), (1, 0)])  33.6 us
    all_to_all x2, blocking collectives, body(): fields.append(lax.all_to_all(before, 'pencil', 0, 0, tiled=True))  33.6 us
    pallas_call x2, Pallas kernels, body(): pl.pallas_call(functools.partial(columns_kernel, special), grid_spec=pltp...  30.4 us
    unnamed x37, local copies, waits for them, and re-layouts  13.7 us
    all_to_all x1, waiting for transfers between devices, body(): fields.append(lax.all_to_all(before, 'pencil', 0, 0, tiled=True))  11.2 us
    ppermute x1, waiting for transfers between devices, body(): before = out[0, 1] + lax.ppermute(second, 'depth', [(0, 1), (1, 0)])  11 us
    pallas_call x1, Pallas kernels, body(): pl.pallas_call(functools.partial(rows_kernel, pencils, width), grid=(part...  8.69 us
  transfers between devices with their start and end apart: 8, of which 6 were waited for; matrix products, arithmetic and copies ran while one was open for 3% of the time, Pallas kernels for 9%

profile of v3, /device:TPU:0, one launch (start us, length us, event | category | flops | bytes accessed | tf_op | source)
XLA Modules:
  0.0 271.9 jit_solution(4662737565641083311)
XLA Ops:
  7.3 5.8 %shard_map.164 = (f32[1,4,128,128]{3,2,1,0:T(8,128)S(1)}, f32[3,4,128,128]{3,2,1,0:T(8,128)S(1)}) custom-call(s32[3]{0:T(128)S(1)} %add_add_fusion.1.where_ref, bf16[2,2,2048,512]{3,2,1,0:T(8,128)(2,1)} %kern_ref.3), custom_call_target="tpu_custom_call" | custom-call | flops 1048576 | bytes 2097152 | tf_op jit(solution)/shard_map/pallas_call | solution.py:405
  13.1 5.1 %collective-permute-start.1 = (f32[3,4,128,128]{3,2,1,0:T(8,128)S(1)}, f32[3,4,128,128]{3,2,1,0:T(8,128)}, u32[]{:S(2)}, u32[]{:S(2)}) collective-permute-start(f32[3,4,128,128]{3,2,1,0:T(8,128)S(1)} %get-tuple-element.18), channel_id=1, source_target_pairs={{0,12},{4,8},{8,4},{12,0},{1,13},{5,9},{9,5},{13,1},{2,14},{6,10},... | collective-permute-start | bytes 2359304 | tf_op jit(solution)/shard_map/ppermute | solution.py:423
  18.9 2.0 convert_reduce_fusion
  22.4 8.7 %shard_map.163 = (f32[4,2,512,128]{3,2,1,0:T(8,128)S(1)}, f32[4,2,512,128]{3,2,1,0:T(8,128)S(1)}) custom-call(f32[1]{0:T(128)} %bitcast.1.offset_ref, f32[1,1,512,2048]{3,2,1,0:T(8,128)} %in_ref.2, bf16[8,512,256]{2,1,0:T(8,128)(2,1)} %constant.59.clone.high_ref, bf16[8,512,256]{2,1,0:T(8,128)(2,1)} %constant.60.clone.low_ref), custom_call_target="tpu_custom_call" | custom-call | flops 6442450944 | bytes 12582912 | tf_op jit(solution)/shard_map/pallas_call | solution.py:428
  32.5 1.9 broadcast_select_fusion.edge_ref
  34.4 2.3 collective-permute-done.1
  36.8 2.3 pad_maximum_fusion
  39.1 71.6 %all_to_all.25.in_ref = f32[4,2,512,128]{3,2,1,0:T(8,128)} all-to-all(f32[4,2,512,128]{3,2,1,0:T(8,128)S(1)} %get-tuple-element.16), channel_id=1, replica_groups=mesh['grp'=2,'pencil'=4,'depth'=2,'mem'=2] {'pencil'}, dimensions={0} | all-to-all | bytes 4194304 | tf_op jit(solution)/shard_map/all_to_all | solution.py:443
  110.7 3.8 %all-to-all-start = ((f32[4,2,512,128]{3,2,1,0:T(8,128)}), f32[4,2,512,128]{3,2,1,0:T(8,128)S(1)}, u32[]{:S(2)}, u32[]{:S(2)}) async-start(f32[4,2,512,128]{3,2,1,0:T(8,128)} %copy-done.5), calls=%async_computation | async-start | bytes 4194304 | tf_op jit(solution)/shard_map/all_to_all | solution.py:443
  114.5 1.6 copy-done.4
  118.7 15.9 %shard_map.165 = f32[2,1,4,2,256,128]{5,4,3,2,1,0:T(8,128)S(1)} custom-call(s32[3]{0:T(128)S(1)} %add_add_fusion.where_ref, f32[4,2,512,128]{3,2,1,0:T(8,128)S(1)} %copy-done.4, bf16[2,2,2048,512]{3,2,1,0:T(8,128)(2,1)} %kern_ref.3, f32[4,4,4,128,128]{4,3,2,1,0:T(8,128)} %bitcast.36, f32[2,16,128,128]{3,2,1,0:T(8,128)} %broadcast_select_fusion.edge_ref, ...), custom_call_target="tpu_custom_call" | custom-call | flops 1610612736 | bytes 16777216 | tf_op jit(solution)/shard_map/pallas_call | solution.py:488
  134.7 1.6 collective-permute-start.2
  136.3 22.2 %collective-permute-done.2 = f32[4,2,256,128]{3,2,1,0:T(8,128)S(1)} collective-permute-done((f32[4,2,256,128]{3,2,1,0:T(8,128)S(1)}, f32[4,2,256,128]{3,2,1,0:T(8,128)S(1)}, u32[]{:S(2)}, u32[]{:S(2)}) %collective-permute-start.2) | collective-permute-done | bytes 1048608 | tf_op jit(solution)/shard_map/ppermute | solution.py:528
  159.5 2.1 all-to-all-done.in_ref
  163.0 1.6 copy-done.3
  167.2 14.4 %shard_map.166 = f32[2,2,4,2,128,128]{5,4,3,2,1,0:T(8,128)S(1)} custom-call(s32[3]{0:T(128)S(1)} %add_add_fusion.where_ref, f32[4,2,512,128]{3,2,1,0:T(8,128)S(1)} %copy-done.3, bf16[2,2,2048,512]{3,2,1,0:T(8,128)(2,1)} %kern_ref.3, f32[4,4,4,128,128]{4,3,2,1,0:T(8,128)} %bitcast.37, f32[2,16,128,128]{3,2,1,0:T(8,128)} %broadcast_select_fusion.edge_ref, ...), custom_call_target="tpu_custom_call" | custom-call | flops 1610612736 | bytes 16777216 | tf_op jit(solution)/shard_map/pallas_call | solution.py:488
  184.0 11.4 %collective-permute-done.3 = f32[4,2,128,128]{3,2,1,0:T(8,128)S(1)} collective-permute-done((f32[4,2,128,128]{3,2,1,0:T(8,128)S(1)}, f32[4,2,128,128]{3,2,1,0:T(8,128)S(1)}, u32[]{:S(2)}, u32[]{:S(2)}) %collective-permute-start.3) | collective-permute-done | bytes 524320 | tf_op jit(solution)/shard_map/ppermute | solution.py:528
  195.5 16.2 %all_to_all.26.refs_1_ = f32[4,2,128,128]{3,2,1,0:T(8,128)} all-to-all(f32[4,2,128,128]{3,2,1,0:T(8,128)S(1)} %fusion.2), channel_id=1, replica_groups=mesh['grp'=2,'pencil'=4,'depth'=2,'mem'=2] {'pencil'}, dimensions={0} | all-to-all | bytes 1048576 | tf_op jit(solution)/shard_map/all_to_all | solution.py:531
  211.6 3.5 %all-to-all-start.2 = ((f32[4,2,256,128]{3,2,1,0:T(8,128)}), f32[4,2,256,128]{3,2,1,0:T(8,128)S(1)}, u32[]{:S(2)}, u32[]{:S(2)}) async-start(f32[4,2,256,128]{3,2,1,0:T(8,128)} %fusion), calls=%async_computation.2 | async-start | bytes 2097152 | tf_op jit(solution)/shard_map/all_to_all | solution.py:486
  216.7 11.0 %collective-permute-done.4 = f32[4,2,128,128]{3,2,1,0:T(8,128)S(1)} collective-permute-done((f32[4,2,128,128]{3,2,1,0:T(8,128)}, f32[4,2,128,128]{3,2,1,0:T(8,128)S(1)}, u32[]{:S(2)}, u32[]{:S(2)}) %collective-permute-start.4) | collective-permute-done | bytes 524320 | tf_op jit(solution)/shard_map/ppermute | solution.py:532
  228.6 11.2 %all-to-all-done.2.refs_0_ = f32[4,2,256,128]{3,2,1,0:T(8,128)S(1)} async-done(((f32[4,2,256,128]{3,2,1,0:T(8,128)}), f32[4,2,256,128]{3,2,1,0:T(8,128)S(1)}, u32[]{:S(2)}, u32[]{:S(2)}) %all-to-all-start.2) | async-done | bytes 1048608 | tf_op jit(solution)/shard_map/all_to_all | solution.py:486
  239.7 17.4 %all_to_all.27.refs_2_ = f32[4,2,128,128]{3,2,1,0:T(8,128)S(1)} all-to-all(f32[4,2,128,128]{3,2,1,0:T(8,128)} %fusion.1), channel_id=1, replica_groups=mesh['grp'=2,'pencil'=4,'depth'=2,'mem'=2] {'pencil'}, dimensions={0} | all-to-all | bytes 1048576 | tf_op jit(solution)/shard_map/all_to_all | solution.py:533
  258.2 1.6 copy-done.16
  259.8 5.3 %shard_map.167 = f32[1,256,2048]{2,1,0:T(8,128)} custom-call(f32[4,2,256,128]{3,2,1,0:T(8,128)S(1)} %all-to-all-done.2.refs_0_, f32[4,2,128,128]{3,2,1,0:T(8,128)S(1)} %copy-done.11, f32[4,2,128,128]{3,2,1,0:T(8,128)S(1)} %all_to_all.27.refs_2_, bf16[8,512,256]{2,1,0:T(8,128)(2,1)S(1)} %copy-done.16, bf16[8,512,256]{2,1,0:T(8,128)(2,1)} %constant.69.clone.refs_4_), custom_call_target="tpu_custom_call" | custom-call | flops 3221225472 | bytes 8388608 | tf_op jit(solution)/shard_map/pallas_call | solution.py:536
  (56 shorter events, 16.7 us)
Async XLA Ops:
  6.5 15.2 %copy-start = (f32[8,1]{0,1:T(1,128)S(1)}, f32[8,1]{0,1:T(1,128)}, u32[]{:S(2)}) copy-start(f32[8,1]{0,1:T(1,128)} %param.18) | copy-start | bytes 100
  6.5 108.0 %all-gather.3.cloned.1.call-start = ((), (), s32[]{:S(2)}) async-start(), calls=%async_computation.5 | async-start | bytes 5242880 | tf_op jit(solution)/shard_map/all_gather | solution.py:456
  7.3 15.1 %copy-start.17 = (f32[2]{0:T(128)S(1)}, f32[2]{0:T(128)}, u32[]{:S(2)}) copy-start(f32[2]{0:T(128)} %constant.61.clone) | copy-start | bytes 28
  13.1 23.7 %collective-permute-start.1 = (f32[3,4,128,128]{3,2,1,0:T(8,128)S(1)}, f32[3,4,128,128]{3,2,1,0:T(8,128)}, u32[]{:S(2)}, u32[]{:S(2)}) collective-permute-start(f32[3,4,128,128]{3,2,1,0:T(8,128)S(1)} %get-tuple-element.18), channel_id=1, source_target_pairs={{0,12},{4,8},{8,4},{12,0},{1,13},{5,9},{9,5},{13,1},{2,14},{6,10},... | collective-permute-start | bytes 2359304 | tf_op jit(solution)/shard_map/ppermute | solution.py:423
  18.2 16.2 %collective-permute-start = (f32[1,4,128,128]{3,2,1,0:T(8,128)S(1)}, f32[1,4,128,128]{3,2,1,0:T(8,128)S(1)}, u32[]{:S(2)}, u32[]{:S(2)}) collective-permute-start(f32[1,4,128,128]{3,2,1,0:T(8,128)S(1)} %get-tuple-element.17), channel_id=1, source_target_pairs={{0,0},{4,12},{8,8},{12,4},{1,1},{5,13},{9,9},{13,5},{2,2},{6,14},{... | collective-permute-start | bytes 786440 | tf_op jit(solution)/shard_map/ppermute | solution.py:421
  31.1 1.4 copy-start.5
  110.7 3.9 %copy-start.1 = (f32[16,128,128]{2,1,0:T(8,128)S(1)}, f32[16,128,128]{2,1,0:T(8,128)}, u32[]{:S(2)}) copy-start(f32[16,128,128]{2,1,0:T(8,128)} %constant.62.clone.turns_ref.late_ref) | copy-start | bytes 3145732
  110.7 3.9 %copy-start.6 = (bf16[256,256]{1,0:T(8,128)(2,1)S(1)}, bf16[256,256]{1,0:T(8,128)(2,1)}, u32[]{:S(2)}) copy-start(bf16[256,256]{1,0:T(8,128)(2,1)} %constant.63.clone.fh_ref) | copy-start | bytes 393220
  110.7 3.9 %copy-start.7 = (bf16[256,256]{1,0:T(8,128)(2,1)S(1)}, bf16[256,256]{1,0:T(8,128)(2,1)}, u32[]{:S(2)}) copy-start(bf16[256,256]{1,0:T(8,128)(2,1)} %constant.64.clone.fl_ref) | copy-start | bytes 393220
  110.7 3.9 %copy-start.8 = (bf16[256,256]{1,0:T(8,128)(2,1)S(1)}, bf16[256,256]{1,0:T(8,128)(2,1)}, u32[]{:S(2)}) copy-start(bf16[256,256]{1,0:T(8,128)(2,1)} %constant.65.clone.ih_ref) | copy-start | bytes 393220
  110.7 51.0 %all-to-all-start = ((f32[4,2,512,128]{3,2,1,0:T(8,128)}), f32[4,2,512,128]{3,2,1,0:T(8,128)S(1)}, u32[]{:S(2)}, u32[]{:S(2)}) async-start(f32[4,2,512,128]{3,2,1,0:T(8,128)} %copy-done.5), calls=%async_computation | async-start | bytes 4194304 | tf_op jit(solution)/shard_map/all_to_all | solution.py:443
  114.5 1.6 copy-start.4
  116.1 0.9 copy-start.9
  117.0 0.8 copy-start.12
  117.9 0.8 copy-start.14
  134.7 23.8 %collective-permute-start.2 = (f32[4,2,256,128]{3,2,1,0:T(8,128)S(1)}, f32[4,2,256,128]{3,2,1,0:T(8,128)S(1)}, u32[]{:S(2)}, u32[]{:S(2)}) collective-permute-start(f32[4,2,256,128]{3,2,1,0:T(8,128)S(1)} %slice_bitcast_fusion), channel_id=1, source_target_pairs={{0,2},{2,0},{1,3},{3,1},{4,6},{6,4},{5,7},{7,5},{8,10},{10,8},{9,1... | collective-permute-start | bytes 3145736 | tf_op jit(solution)/shard_map/ppermute | solution.py:528
  161.6 1.4 copy-start.2
  163.0 1.6 copy-start.3
  164.6 0.9 copy-start.10
  182.5 12.9 %collective-permute-start.3 = (f32[4,2,128,128]{3,2,1,0:T(8,128)S(1)}, f32[4,2,128,128]{3,2,1,0:T(8,128)S(1)}, u32[]{:S(2)}, u32[]{:S(2)}) collective-permute-start(f32[4,2,128,128]{3,2,1,0:T(8,128)S(1)} %get-tuple-element.25), channel_id=1, source_target_pairs={{0,2},{2,0},{1,3},{3,1},{4,6},{6,4},{5,7},{7,5},{8,10},{10,8},{9,1... | collective-permute-start | bytes 1572872 | tf_op jit(solution)/shard_map/ppermute | solution.py:528
  211.6 28.1 %all-to-all-start.2 = ((f32[4,2,256,128]{3,2,1,0:T(8,128)}), f32[4,2,256,128]{3,2,1,0:T(8,128)S(1)}, u32[]{:S(2)}, u32[]{:S(2)}) async-start(f32[4,2,256,128]{3,2,1,0:T(8,128)} %fusion), calls=%async_computation.2 | async-start | bytes 2097152 | tf_op jit(solution)/shard_map/all_to_all | solution.py:486
  215.1 12.5 %collective-permute-start.4 = (f32[4,2,128,128]{3,2,1,0:T(8,128)}, f32[4,2,128,128]{3,2,1,0:T(8,128)S(1)}, u32[]{:S(2)}, u32[]{:S(2)}) collective-permute-start(f32[4,2,128,128]{3,2,1,0:T(8,128)} %get-tuple-element.24), channel_id=1, source_target_pairs={{0,2},{2,0},{1,3},{3,1},{4,6},{6,4},{5,7},{7,5},{8,10},{10,8},{9,1... | collective-permute-start | bytes 1572872 | tf_op jit(solution)/shard_map/ppermute | solution.py:532
  257.1 1.0 copy-start.11
  258.2 1.6 copy-start.16
  (2 other events, 1.7 us)
Sparse Core Ops, SparseCore 0:
  39.2 55.1 all-gather.2

commit v4 on v3

--- a/solution.py
+++ b/solution.py
@@ -205,36 +205,44 @@
                     outs[place][pencil, c] = total[:, begin : begin + HALF]
 
 
-def mirror_kernel(where_ref, in_ref, zero_ref, *rest_refs):
-    per = in_ref.shape[2] // INNER
-
-    def swapped(zero, shape, axis):
-        to = lax.broadcasted_iota(jnp.int32, shape, axis)
-        begin = lax.broadcasted_iota(jnp.int32, shape, 1 - axis)
-        total = jnp.where(zero, INNER, INNER - 1)
-        return jnp.where((to + begin == total) | (zero & (to + begin == 0)), 1.0, 0.0).astype(bf16)
-
-    swap = swapped(where_ref[1] + pl.program_id(0) == 0, (INNER, INNER), 0)
+def swapped(zero, shape, axis):
+    total = lax.broadcasted_iota(jnp.int32, shape, 0) + lax.broadcasted_iota(jnp.int32, shape, 1)
+    wanted = jnp.where(zero, INNER, INNER - 1)
+    also = jnp.where(zero, 0, INNER - 1)
+    return jnp.where((total == wanted) | (total == also), 1.0, 0.0).astype(bf16)
+
+
+def mirror_kernel(share, where_ref, *refs):
+    ins, zero_ref, rest_refs = refs[:share], refs[share], refs[share + 1 :]
+    per = ins[0].shape[2] // INNER
     plain = swapped(where_ref[1] < 0, (INNER, HALF), 1)
-    for j in range(per):
-        turn = swapped(where_ref[2] == 0, (INNER, HALF), 1) if j == 0 else plain
-        turned = [dot(in_ref[c, :, j * INNER : (j + 1) * INNER], turn) for c in range(2)]
-        value = dot(swap, jnp.concatenate(turned, axis=1).astype(bf16))
-        if j == 0:
-            zero_ref[0, 0] = value
-        else:
-            rest_refs[0][per - 1 - j, 0] = value
-
-
-def columns_kernel(special, where_ref, in_ref, kern_ref, mirror_ref, edge_ref, swap_ref, pick_ref,
-                   turns_ref, late_ref, fh_ref, fl_ref, ih_ref, il_ref, out_ref, pieces, waves):
+    edge = swapped(where_ref[2] == 0, (INNER, HALF), 1)
+    for u in range(share):
+        swap = swapped(where_ref[1] + u == 0, (INNER, INNER), 0)
+        for j in range(per):
+            turn = edge if j == 0 else plain
+            turned = [dot(ins[u][c, :, j * INNER : (j + 1) * INNER], turn) for c in range(2)]
+            value = dot(swap, jnp.concatenate(turned, axis=1).astype(bf16))
+            if j == 0:
+                zero_ref[0, u] = value
+            else:
+                rest_refs[0][per - 1 - j, u] = value
+
+
+def columns_kernel(special, where_ref, in_ref, kern_ref, mirror_ref, edge_ref,
+                   turns_ref, late_ref, table_ref, out_ref, pieces, waves):
     part_rows = in_ref.shape[2]
-    depths, splits, pencils, _, split_rows, lanes = out_ref.shape
-    out_rows = splits * split_rows
+    depths, pencils, _, out_rows, lanes = out_ref.shape
     share = mirror_ref.shape[1]
     steps = RADIX // share
     mine = where_ref[0]
     now = pl.program_id(0)
+    from_lane = lax.broadcasted_iota(jnp.int32, (kern_ref.shape[2], lanes), 0)
+    to_lane = lax.broadcasted_iota(jnp.int32, (kern_ref.shape[2], lanes), 1)
+    wanted = to_lane + jnp.where(to_lane < HALF, 0, HALF)
+    pick = jnp.where(from_lane == wanted, 0.5, 0.0).astype(bf16)
+    zero_swap = swapped(mine >= 0, (INNER, INNER), 0)
+    plain_swap = swapped(mine < 0, (INNER, INNER), 0)
 
     def forward(b, carry):
         values = []
@@ -257,7 +265,7 @@
         re, im = pieces[r, :INNER], pieces[r, INNER:]
         c, s = turns_ref[u, :, 0:1], turns_ref[u, :, 1:2]
         high, low = split_value(jnp.concatenate([re * c + im * s, im * c - re * s], axis=0))
-        return dot(fh_ref[...], high) + dot(fh_ref[...], low) + dot(fl_ref[...], high)
+        return dot(table_ref[0], high) + dot(table_ref[0], low) + dot(table_ref[1], high)
 
     def finish(r, u, got):
         re, im = got[:INNER], got[INNER:]
@@ -267,13 +275,13 @@
         for c in range(2):
             other = [tile[:, c * HALF : (c + 1) * HALF] for tile in tiles]
             other = jnp.concatenate(other, axis=1) if len(other) > 1 else other[0]
-            own = dot(kern_ref[c, rows, :], pick_ref[...])
+            own = dot(kern_ref[c, rows, :], pick)
             parts.append(own + 0.5 * other if c == 0 else own - 0.5 * other)
         kr, ki = parts
         if special:
             other = lax.rem(RADIX - r, RADIX)
             high, low = split_value(waves[other])
-            swap = swap_ref[jnp.where(r == 0, 0, 1)]
+            swap = jnp.where(r == 0, zero_swap.astype(f32), plain_swap.astype(f32)).astype(bf16) if u == 0 else plain_swap
             ore = dot(swap, high[:INNER]) + dot(swap, low[:INNER])
             oim = -(dot(swap, high[INNER:]) + dot(swap, low[INNER:]))
             mask = (lax.broadcasted_iota(jnp.int32, (INNER, lanes), 1) == 0) & (where_ref[2] == 0)
@@ -286,7 +294,7 @@
             sr, si = re * kr - im * ki, re * ki + im * kr
         spectrum = jnp.concatenate([sr, si], axis=0)
         high, low = split_value(spectrum)
-        got = dot(ih_ref[...], high) + dot(ih_ref[...], low) + dot(il_ref[...], high)
+        got = dot(table_ref[2], high) + dot(table_ref[2], low) + dot(table_ref[3], high)
         re, im = got[:INNER], got[INNER:]
         c, s = late_ref[u, :, 0:1], late_ref[u, :, 1:2]
         pieces[r, :INNER] = re * c - im * s
@@ -308,18 +316,25 @@
             r = now * share + u
             finish(r, u, wave(r, u))
 
+    slots = [lax.rem(d - mine + depths, depths) for d in range(depths)]
+
     def backward(b, carry):
         at = pl.ds(pl.multiple_of(b * 8, 8), 8)
         also = pl.ds(pl.multiple_of(INNER + b * 8, 8), 8)
         values = [(pieces[r, at, :], pieces[r, also, :]) for r in range(RADIX)]
         for n, (re, im) in enumerate(transform(values, 1)):
-            x = n * INNER + b * 8
-            pencil = x // (out_rows * depths)
-            depth = lax.rem(x // out_rows - mine + depths, depths)
-            part = lax.rem(x, out_rows) // split_rows
-            put = pl.ds(pl.multiple_of(lax.rem(x, split_rows), 8), 8)
-            out_ref[depth, part, pencil, 0, put, :] = re
-            out_ref[depth, part, pencil, 1, put, :] = im
+            if out_rows % INNER == 0:
+                part, begin = divmod(n * INNER, out_rows)
+                pencil, depth = divmod(part, depths)
+                depth = slots[depth]
+                put = pl.ds(pl.multiple_of(begin + b * 8, 8), 8)
+            else:
+                x = n * INNER + b * 8
+                pencil = x // (out_rows * depths)
+                depth = lax.rem(x // out_rows - mine + depths, depths)
+                put = pl.ds(pl.multiple_of(lax.rem(x, out_rows), 8), 8)
+            out_ref[depth, pencil, 0, put, :] = re
+            out_ref[depth, pencil, 1, put, :] = im
         return carry
 
     @pl.when(now == pl.num_programs(0) - 1)
@@ -396,28 +411,25 @@
     local = layer_kernel[0] - lax.axis_index("depth") * kern_count
     share = RADIX // sharers
     first = lax.axis_index(("grp", "mem")) * share
-    index = np.arange(INNER)
-    swaps = np.zeros((2, INNER, INNER), np.float32)
-    swaps[0, index, (INNER - index) % INNER] = 1.0
-    swaps[1, index, INNER - 1 - index] = 1.0
-    swaps = jnp.asarray(swaps.astype(bf16))
     groups = [1] if per == 1 else [1, per - 1]
     moved = pl.pallas_call(
-        mirror_kernel,
+        functools.partial(mirror_kernel, share),
         grid_spec=pltpu.PrefetchScalarGridSpec(
             num_scalar_prefetch=1,
-            grid=(share,),
+            grid=(1,),
             in_specs=[
                 pl.BlockSpec(
-                    (None, 2, INNER, per * INNER), lambda i, w: (w[0], 0, lax.rem(RADIX - w[1] - i, RADIX), 0)
-                ),
+                    (None, 2, INNER, per * INNER),
+                    lambda i, w, u=u: (w[0], 0, lax.rem(RADIX - w[1] - u, RADIX), 0),
+                )
+                for u in range(share)
             ],
-            out_specs=[pl.BlockSpec((g, 1, INNER, INNER), lambda i, w: (0, i, 0, 0)) for g in groups],
+            out_specs=[pl.BlockSpec((g, share, INNER, INNER), lambda i, w: (0, 0, 0, 0)) for g in groups],
         ),
         out_shape=[jax.ShapeDtypeStruct((g, share, INNER, INNER), f32) for g in groups],
         compiler_params=params(),
         cost_estimate=pl.CostEstimate(flops=1 << 20, bytes_accessed=2 << 20, transcendentals=0),
-    )(jnp.stack([local, first, pencil]), kernel_spectra)
+    )(jnp.stack([local, first, pencil]), *[kernel_spectra] * share)
     mirrored = lax.ppermute(moved[0], "pencil", [(p, (pencils - p) % pencils) for p in range(pencils)])
     if per > 1:
         rest = lax.ppermute(moved[1], "pencil", [(p, pencils - 1 - p) for p in range(pencils)])
@@ -457,15 +469,11 @@
 
     column, column_turns = column_tables()
     column_turns = jnp.asarray(column_turns)
-    tables = halves(column) + halves(column.T)
-    pick = np.zeros((width * INNER, lanes), np.float32)
-    for j in range(width):
-        pick[j * INNER + np.arange(HALF), j * HALF + np.arange(HALF)] = 0.5
-    pick = jnp.asarray(pick.astype(bf16))
+    tables = jnp.stack(halves(column) + halves(column.T))
     two = depths == 2
     mine = lax.axis_index("depth") if two else jnp.int32(0)
     where = jnp.stack([mine, local, pencil])
-    fields, counts = [], []
+    fields = []
     before = None
     for k in range(chunks):
         special = k == 0
@@ -478,9 +486,6 @@
             return jnp.maximum(i - steps, 0) if special else i
 
         here = arrived[k]
-        splits = 2 if two and k == chunks - 1 else 1
-        counts.append(splits)
-        split_rows = out_rows // splits
         if before is not None:
             here, before = lax.optimization_barrier((here, before))
             fields.append(lax.all_to_all(before, "pencil", 0, 0, tiled=True))
@@ -502,39 +507,31 @@
                         edge_block,
                         (lambda i, w, late=late: (0, late(i), 0, 0)) if special else (lambda i, w: (0, 0, 0, 0)),
                     ),
-                    pl.BlockSpec((2, INNER, INNER), lambda i, w: (0, 0, 0)),
-                    pl.BlockSpec(pick.shape, lambda i, w: (0, 0)),
                 ]
                 + [pl.BlockSpec((share, INNER, INNER), lambda i, w, early=early: (early(i), 0, 0))]
                 + [pl.BlockSpec((share, INNER, INNER), lambda i, w, late=late: (late(i), 0, 0))]
-                + [pl.BlockSpec((256, 256), lambda i, w: (0, 0))] * 4,
-                out_specs=pl.BlockSpec(
-                    (depths, splits, pencils, 2, split_rows, lanes), lambda i, w: (0, 0, 0, 0, 0, 0)
-                ),
+                + [pl.BlockSpec((4, 256, 256), lambda i, w: (0, 0, 0))],
+                out_specs=pl.BlockSpec((depths, pencils, 2, out_rows, lanes), lambda i, w: (0, 0, 0, 0, 0)),
                 scratch_shapes=[
                     pltpu.VMEM((RADIX, 256, lanes), f32),
                     pltpu.VMEM((RADIX if special else 1, 256, lanes), f32),
                 ],
             ),
-            out_shape=jax.ShapeDtypeStruct((depths, splits, pencils, 2, split_rows, lanes), f32),
+            out_shape=jax.ShapeDtypeStruct((depths, pencils, 2, out_rows, lanes), f32),
             compiler_params=params(),
             cost_estimate=pl.CostEstimate(
                 flops=12 * RADIX * 256 * 256 * lanes, bytes_accessed=16 << 20, transcendentals=0
             ),
-        )(where, here, kernel_spectra, mirrored, edge, swaps, pick, column_turns, column_turns, *tables)
-        if not two:
-            before = lax.psum_scatter(out[:, 0], "depth", scatter_dimension=0, tiled=False)
-            continue
-        before = out[0, 0] + lax.ppermute(out[1, 0], "depth", [(0, 1), (1, 0)])
-        if splits == 2:
-            second, before = lax.optimization_barrier((out[1, 1], before))
-            fields.append(lax.all_to_all(before, "pencil", 0, 0, tiled=True))
-            before = out[0, 1] + lax.ppermute(second, "depth", [(0, 1), (1, 0)])
+        )(where, here, kernel_spectra, mirrored, edge, column_turns, column_turns, tables)
+        if two:
+            before = out[0] + lax.ppermute(out[1], "depth", [(0, 1), (1, 0)])
+        else:
+            before = lax.psum_scatter(out, "depth", scatter_dimension=0, tiled=False)
     fields.append(lax.all_to_all(before, "pencil", 0, 0, tiled=True))
 
     back_high, back_low = halves(inverse_row_tables())
     return pl.pallas_call(
-        functools.partial(fields_kernel, pencils, width, counts),
+        functools.partial(fields_kernel, pencils, width, [1] * chunks),
         in_specs=[vmem] * (len(fields) + 2),
         out_specs=vmem,
         out_shape=jax.ShapeDtypeStruct((1, out_rows, LENGTH), f32),

time: 273 us -> 243 us (0.89)
  local copies, waits for them, and re-layouts: 15.5 us -> 6.04 us
  Pallas kernels: 50.1 us -> 43.6 us
  waiting for transfers between devices: 60.2 us -> 53.8 us
  blocking collectives: 105 us -> 99.9 us
    all_to_all x1, waiting for transfers between devices: 11.2 us -> 0.01 us  [body(): fields.append(lax.all_to_all(before, 'pencil', 0, 0, tiled=True))]
    unnamed x37 -> x17, local copies, waits for them, and re-layouts: 13.7 us -> 5.05 us
    pallas_call x2, Pallas kernels: 30.4 us -> 23.8 us  [body(): pl.pallas_call(functools.partial(columns_kernel, special), grid_spec=pltp...]
    all_to_all x2 -> x1, blocking collectives: 33.6 us -> 28.3 us  [body(): fields.append(lax.all_to_all(before, 'pencil', 0, 0, tiled=True))]
    all_to_all x1, waiting for transfers between devices: 2.12 us -> 6.66 us  [body(): lax.all_to_all(part, 'pencil', 0, 0, tiled=True)]
    ppermute x3 -> x2, waiting for transfers between devices: 44.6 us -> 44.8 us  [body(): before = out[0] + lax.ppermute(out[1], 'depth', [(0, 1), (1, 0)])]
  transfers between devices with their start and end apart: 8 -> 7, of which waited for: 6 -> 4; matrix products, arithmetic and copies ran while one was open for 3% -> 3% of each run, Pallas kernels for 9% -> 13%
where the time goes in v4:
time: 243 us
  blocking collectives  99.9 us (41%)
  waiting for transfers between devices  53.8 us (22%)
  Pallas kernels  43.6 us (18%)
  starting transfers between devices  16.9 us (7%)
  between operations  14.9 us (6%)
  other arithmetic  7.63 us (3%)
  local copies, waits for them, and re-layouts  6.04 us (2%)
    all_to_all x1, blocking collectives, body(): lax.all_to_all(part, 'pencil', 0, 0, tiled=True)  71.6 us
    ppermute x2, waiting for transfers between devices, body(): before = out[0] + lax.ppermute(out[1], 'depth', [(0, 1), (1, 0)])  44.8 us
    all_to_all x1, blocking collectives, body(): fields.append(lax.all_to_all(before, 'pencil', 0, 0, tiled=True))  28.3 us
    pallas_call x2, Pallas kernels, body(): pl.pallas_call(functools.partial(columns_kernel, special), grid_spec=pltp...  23.8 us
    pallas_call x1, Pallas kernels, body(): pl.pallas_call(functools.partial(rows_kernel, pencils, width), grid=(part...  8.69 us
    all_to_all x1, waiting for transfers between devices, body(): lax.all_to_all(part, 'pencil', 0, 0, tiled=True)  6.66 us
    pallas_call x1, Pallas kernels, body(): pl.pallas_call(functools.partial(fields_kernel, pencils, width, [1] * chu...  5.67 us
    pallas_call x1, Pallas kernels, body(): pl.pallas_call(functools.partial(mirror_kernel, share), grid_spec=pltpu.P...  5.44 us
  transfers between devices with their start and end apart: 7, of which 4 were waited for; matrix products, arithmetic and copies ran while one was open for 3% of the time, Pallas kernels for 13%

profile of v4, /device:TPU:0, one launch (start us, length us, event | category | flops | bytes accessed | tf_op | source)
XLA Modules:
  0.0 242.7 jit_solution(1756163829003935542)
XLA Ops:
  7.3 5.4 %shard_map.146 = (f32[1,4,128,128]{3,2,1,0:T(8,128)S(1)}, f32[3,4,128,128]{3,2,1,0:T(8,128)S(1)}) custom-call(s32[3]{0:T(128)S(1)} %add_add_fusion.1.where_ref, bf16[2,2,2048,512]{3,2,1,0:T(8,128)(2,1)} %kern_ref.3, bf16[2,2,2048,512]{3,2,1,0:T(8,128)(2,1)} %kern_ref.3, bf16[2,2,2048,512]{3,2,1,0:T(8,128)(2,1)} %kern_ref.3, bf16[2,2,2048,512]{3,2,1,0:T(8,128)(2,1)} %kern_ref.3), custom_call_target="tpu_custom_call" | custom-call | flops 1048576 | bytes 2097152 | tf_op jit(solution)/shard_map/pallas_call | solution.py:415
  12.7 5.1 %collective-permute-start.1 = (f32[3,4,128,128]{3,2,1,0:T(8,128)S(1)}, f32[3,4,128,128]{3,2,1,0:T(8,128)}, u32[]{:S(2)}, u32[]{:S(2)}) collective-permute-start(f32[3,4,128,128]{3,2,1,0:T(8,128)S(1)} %get-tuple-element.16), channel_id=1, source_target_pairs={{0,12},{4,8},{8,4},{12,0},{1,13},{5,9},{9,5},{13,1},{2,14},{6,10},... | collective-permute-start | bytes 2359304 | tf_op jit(solution)/shard_map/ppermute | solution.py:435
  18.5 2.0 convert_reduce_fusion
  22.1 8.7 %shard_map.145 = (f32[4,2,512,128]{3,2,1,0:T(8,128)S(1)}, f32[4,2,512,128]{3,2,1,0:T(8,128)S(1)}) custom-call(f32[1]{0:T(128)} %bitcast.1.offset_ref, f32[1,1,512,2048]{3,2,1,0:T(8,128)} %in_ref.1, bf16[8,512,256]{2,1,0:T(8,128)(2,1)} %constant.54.clone.high_ref, bf16[8,512,256]{2,1,0:T(8,128)(2,1)} %constant.55.clone.low_ref), custom_call_target="tpu_custom_call" | custom-call | flops 6442450944 | bytes 12582912 | tf_op jit(solution)/shard_map/pallas_call | solution.py:440
  30.8 1.4 copy-done.5
  32.2 1.9 broadcast_select_fusion.edge_ref
  34.1 2.3 collective-permute-done.1
  36.4 2.3 pad_maximum_fusion
  38.8 71.6 %all_to_all.20.in_ref = f32[4,2,512,128]{3,2,1,0:T(8,128)} all-to-all(f32[4,2,512,128]{3,2,1,0:T(8,128)S(1)} %get-tuple-element.14), channel_id=1, replica_groups=mesh['grp'=2,'pencil'=4,'depth'=2,'mem'=2] {'pencil'}, dimensions={0} | all-to-all | bytes 4194304 | tf_op jit(solution)/shard_map/all_to_all | solution.py:455
  110.3 3.7 %all-to-all-start = ((f32[4,2,512,128]{3,2,1,0:T(8,128)}), f32[4,2,512,128]{3,2,1,0:T(8,128)S(1)}, u32[]{:S(2)}, u32[]{:S(2)}) async-start(f32[4,2,512,128]{3,2,1,0:T(8,128)} %copy-done.5), calls=%async_computation | async-start | bytes 4194304 | tf_op jit(solution)/shard_map/all_to_all | solution.py:455
  114.2 1.6 copy-done.2
  115.8 1.0 copy-done.3
  116.8 12.9 %shard_map.147 = f32[2,4,2,256,128]{4,3,2,1,0:T(8,128)S(1)} custom-call(s32[3]{0:T(128)S(1)} %add_add_fusion.where_ref, f32[4,2,512,128]{3,2,1,0:T(8,128)S(1)} %copy-done.2, bf16[2,2,2048,512]{3,2,1,0:T(8,128)(2,1)} %kern_ref.3, f32[4,4,4,128,128]{4,3,2,1,0:T(8,128)} %bitcast.30, f32[2,16,128,128]{3,2,1,0:T(8,128)} %broadcast_select_fusion.edge_ref, ...), custom_call_target="tpu_custom_call" | custom-call | flops 1610612736 | bytes 16777216 | tf_op jit(solution)/shard_map/pallas_call | solution.py:493
  129.8 1.6 collective-permute-start.2
  131.4 22.2 %collective-permute-done.2 = f32[4,2,256,128]{3,2,1,0:T(8,128)S(1)} collective-permute-done((f32[4,2,256,128]{3,2,1,0:T(8,128)S(1)}, f32[4,2,256,128]{3,2,1,0:T(8,128)S(1)}, u32[]{:S(2)}, u32[]{:S(2)}) %collective-permute-start.2) | collective-permute-done | bytes 1048608 | tf_op jit(solution)/shard_map/ppermute | solution.py:527
  153.6 1.1 fusion.1
  154.6 6.7 %all-to-all-done.in_ref = f32[4,2,512,128]{3,2,1,0:T(8,128)S(1)} async-done(((f32[4,2,512,128]{3,2,1,0:T(8,128)}), f32[4,2,512,128]{3,2,1,0:T(8,128)S(1)}, u32[]{:S(2)}, u32[]{:S(2)}) %all-to-all-start) | async-done | bytes 2097184 | tf_op jit(solution)/shard_map/all_to_all | solution.py:455
  161.3 4.2 %all-to-all-start.2 = ((f32[4,2,256,128]{3,2,1,0:T(8,128)}), f32[4,2,256,128]{3,2,1,0:T(8,128)}, u32[]{:S(2)}, u32[]{:S(2)}) async-start(f32[4,2,256,128]{3,2,1,0:T(8,128)} %fusion.1), calls=%async_computation.2 | async-start | bytes 2097152 | tf_op jit(solution)/shard_map/all_to_all | solution.py:491
  165.6 1.0 copy-done.4
  166.6 10.9 %shard_map.148 = f32[2,4,2,256,128]{4,3,2,1,0:T(8,128)S(1)} custom-call(s32[3]{0:T(128)S(1)} %add_add_fusion.where_ref, f32[4,2,512,128]{3,2,1,0:T(8,128)S(1)} %all-to-all-done.in_ref, bf16[2,2,2048,512]{3,2,1,0:T(8,128)(2,1)} %kern_ref.3, f32[4,4,4,128,128]{4,3,2,1,0:T(8,128)} %bitcast.31, f32[2,16,128,128]{3,2,1,0:T(8,128)} %broadcast_select_fusion.edge_ref, ...), custom_call_target="tpu_custom_call" | custom-call | flops 1610612736 | bytes 16777216 | tf_op jit(solution)/shard_map/pallas_call | solution.py:493
  177.6 1.6 collective-permute-start.3
  179.2 22.6 %collective-permute-done.3 = f32[4,2,256,128]{3,2,1,0:T(8,128)S(1)} collective-permute-done((f32[4,2,256,128]{3,2,1,0:T(8,128)S(1)}, f32[4,2,256,128]{3,2,1,0:T(8,128)S(1)}, u32[]{:S(2)}, u32[]{:S(2)}) %collective-permute-start.3) | collective-permute-done | bytes 1048608 | tf_op jit(solution)/shard_map/ppermute | solution.py:527
  201.9 28.3 %all_to_all.21.refs_1_ = f32[4,2,256,128]{3,2,1,0:T(8,128)S(1)} all-to-all(f32[4,2,256,128]{3,2,1,0:T(8,128)S(1)} %fusion), channel_id=1, replica_groups=mesh['grp'=2,'pencil'=4,'depth'=2,'mem'=2] {'pencil'}, dimensions={0} | all-to-all | bytes 2097152 | tf_op jit(solution)/shard_map/all_to_all | solution.py:530
  230.2 5.7 %shard_map.149 = f32[1,256,2048]{2,1,0:T(8,128)} custom-call(f32[4,2,256,128]{3,2,1,0:T(8,128)} %all-to-all-done.2.refs_0_, f32[4,2,256,128]{3,2,1,0:T(8,128)S(1)} %all_to_all.21.refs_1_, bf16[8,512,256]{2,1,0:T(8,128)(2,1)S(1)} %copy-done.6, bf16[8,512,256]{2,1,0:T(8,128)(2,1)} %constant.63.clone.refs_3_), custom_call_target="tpu_custom_call" | custom-call | flops 3221225472 | bytes 8388608 | tf_op jit(solution)/shard_map/pallas_call | solution.py:533
  (32 shorter events, 2.1 us)
Async XLA Ops:
  6.5 14.9 %copy-start = (f32[8,1]{0,1:T(1,128)S(1)}, f32[8,1]{0,1:T(1,128)}, u32[]{:S(2)}) copy-start(f32[8,1]{0,1:T(1,128)} %param.16) | copy-start | bytes 100
  6.5 107.6 %all-gather.3.cloned.1.call-start = ((), (), s32[]{:S(2)}) async-start(), calls=%async_computation.4 | async-start | bytes 5242880 | tf_op jit(solution)/shard_map/all_gather | solution.py:468
  7.3 14.7 %copy-start.7 = (f32[2]{0:T(128)S(1)}, f32[2]{0:T(128)}, u32[]{:S(2)}) copy-start(f32[2]{0:T(128)} %constant.56.clone) | copy-start | bytes 28
  12.7 23.7 %collective-permute-start.1 = (f32[3,4,128,128]{3,2,1,0:T(8,128)S(1)}, f32[3,4,128,128]{3,2,1,0:T(8,128)}, u32[]{:S(2)}, u32[]{:S(2)}) collective-permute-start(f32[3,4,128,128]{3,2,1,0:T(8,128)S(1)} %get-tuple-element.16), channel_id=1, source_target_pairs={{0,12},{4,8},{8,4},{12,0},{1,13},{5,9},{9,5},{13,1},{2,14},{6,10},... | collective-permute-start | bytes 2359304 | tf_op jit(solution)/shard_map/ppermute | solution.py:435
  17.9 16.3 %collective-permute-start = (f32[1,4,128,128]{3,2,1,0:T(8,128)S(1)}, f32[1,4,128,128]{3,2,1,0:T(8,128)S(1)}, u32[]{:S(2)}, u32[]{:S(2)}) collective-permute-start(f32[1,4,128,128]{3,2,1,0:T(8,128)S(1)} %get-tuple-element.15), channel_id=1, source_target_pairs={{0,0},{4,12},{8,8},{12,4},{1,1},{5,13},{9,9},{13,5},{2,2},{6,14},{... | collective-permute-start | bytes 786440 | tf_op jit(solution)/shard_map/ppermute | solution.py:433
  30.8 1.4 copy-start.5
  110.3 3.8 %copy-start.1 = (f32[16,128,128]{2,1,0:T(8,128)S(1)}, f32[16,128,128]{2,1,0:T(8,128)}, u32[]{:S(2)}) copy-start(f32[16,128,128]{2,1,0:T(8,128)} %constant.57.clone.turns_ref.late_ref) | copy-start | bytes 3145732
  110.3 51.0 %all-to-all-start = ((f32[4,2,512,128]{3,2,1,0:T(8,128)}), f32[4,2,512,128]{3,2,1,0:T(8,128)S(1)}, u32[]{:S(2)}, u32[]{:S(2)}) async-start(f32[4,2,512,128]{3,2,1,0:T(8,128)} %copy-done.5), calls=%async_computation | async-start | bytes 4194304 | tf_op jit(solution)/shard_map/all_to_all | solution.py:455
  114.2 1.6 copy-start.2
  115.8 1.0 copy-start.3
  129.8 23.7 %collective-permute-start.2 = (f32[4,2,256,128]{3,2,1,0:T(8,128)S(1)}, f32[4,2,256,128]{3,2,1,0:T(8,128)S(1)}, u32[]{:S(2)}, u32[]{:S(2)}) collective-permute-start(f32[4,2,256,128]{3,2,1,0:T(8,128)S(1)} %slice_bitcast_fusion.2), channel_id=1, source_target_pairs={{0,2},{2,0},{1,3},{3,1},{4,6},{6,4},{5,7},{7,5},{8,10},{10,8},{9,1... | collective-permute-start | bytes 3145736 | tf_op jit(solution)/shard_map/ppermute | solution.py:527
  161.3 40.6 %all-to-all-start.2 = ((f32[4,2,256,128]{3,2,1,0:T(8,128)}), f32[4,2,256,128]{3,2,1,0:T(8,128)}, u32[]{:S(2)}, u32[]{:S(2)}) async-start(f32[4,2,256,128]{3,2,1,0:T(8,128)} %fusion.1), calls=%async_computation.2 | async-start | bytes 2097152 | tf_op jit(solution)/shard_map/all_to_all | solution.py:491
  165.6 1.0 copy-start.4
  177.6 52.6 %copy-start.6 = (bf16[8,512,256]{2,1,0:T(8,128)(2,1)S(1)}, bf16[8,512,256]{2,1,0:T(8,128)(2,1)}, u32[]{:S(2)}) copy-start(bf16[8,512,256]{2,1,0:T(8,128)(2,1)} %constant.62.clone.refs_2_) | copy-start | bytes 6291460
  177.6 24.2 %collective-permute-start.3 = (f32[4,2,256,128]{3,2,1,0:T(8,128)S(1)}, f32[4,2,256,128]{3,2,1,0:T(8,128)S(1)}, u32[]{:S(2)}, u32[]{:S(2)}) collective-permute-start(f32[4,2,256,128]{3,2,1,0:T(8,128)S(1)} %slice_bitcast_fusion), channel_id=1, source_target_pairs={{0,2},{2,0},{1,3},{3,1},{4,6},{6,4},{5,7},{7,5},{8,10},{10,8},{9,1... | collective-permute-start | bytes 3145736 | tf_op jit(solution)/shard_map/ppermute | solution.py:527
Sparse Core Ops, SparseCore 0:
  38.9 55.1 all-gather.2

commit v5 on v4

--- a/solution.py
+++ b/solution.py
@@ -219,10 +219,11 @@
     edge = swapped(where_ref[2] == 0, (INNER, HALF), 1)
     for u in range(share):
         swap = swapped(where_ref[1] + u == 0, (INNER, INNER), 0)
+        rows = [dot(swap, ins[u][c]).astype(bf16) for c in range(2)]
         for j in range(per):
             turn = edge if j == 0 else plain
-            turned = [dot(ins[u][c, :, j * INNER : (j + 1) * INNER], turn) for c in range(2)]
-            value = dot(swap, jnp.concatenate(turned, axis=1).astype(bf16))
+            turned = [dot(rows[c][:, j * INNER : (j + 1) * INNER], turn) for c in range(2)]
+            value = jnp.concatenate(turned, axis=1)
             if j == 0:
                 zero_ref[0, u] = value
             else:

time: 243 us -> 241 us (level)
  Pallas kernels: 43.6 us -> 41 us
    pallas_call x1, Pallas kernels: 5.44 us -> 2.83 us  [body(): pl.pallas_call(functools.partial(mirror_kernel, share), grid_spec=pltpu.P...]
  transfers between devices with their start and end apart: 7 -> 7, of which waited for: 4 -> 4; matrix products, arithmetic and copies ran while one was open for 3% -> 3% of each run, Pallas kernels for 13% -> 14%
where the time goes in v5:
time: 241 us; the launch traced here: 240 us
  blocking collectives  99.8 us (41%)
  waiting for transfers between devices  53.7 us (22%)
  Pallas kernels  41 us (17%)
  starting transfers between devices  17 us (7%)
  between operations  14.9 us (6%)
  other arithmetic  7.63 us (3%)
  local copies, waits for them, and re-layouts  6.04 us (3%)
    all_to_all x1, blocking collectives, body(): lax.all_to_all(part, 'pencil', 0, 0, tiled=True)  71.5 us
    ppermute x2, waiting for transfers between devices, body(): before = out[0] + lax.ppermute(out[1], 'depth', [(0, 1), (1, 0)])  44.7 us
    all_to_all x1, blocking collectives, body(): fields.append(lax.all_to_all(before, 'pencil', 0, 0, tiled=True))  28.3 us
    pallas_call x2, Pallas kernels, body(): pl.pallas_call(functools.partial(columns_kernel, special), grid_spec=pltp...  23.8 us
    pallas_call x1, Pallas kernels, body(): pl.pallas_call(functools.partial(rows_kernel, pencils, width), grid=(part...  8.69 us
    all_to_all x1, waiting for transfers between devices, body(): lax.all_to_all(part, 'pencil', 0, 0, tiled=True)  6.65 us
    pallas_call x1, Pallas kernels, body(): pl.pallas_call(functools.partial(fields_kernel, pencils, width, [1] * chu...  5.67 us
    ppermute x1, starting transfers between devices, body(): lax.ppermute(moved[1], 'pencil', [(p, pencils - 1 - p) for p in range(pen...  5.11 us
  transfers between devices with their start and end apart: 7, of which 4 were waited for; matrix products, arithmetic and copies ran while one was open for 3% of the time, Pallas kernels for 14%

profile of v5, /device:TPU:0, one launch (start us, length us, event | category | flops | bytes accessed | tf_op | source)
XLA Modules:
  0.0 240.1 jit_solution(16438916901628065476)
XLA Ops:
  7.3 2.8 %shard_map.146 = (f32[1,4,128,128]{3,2,1,0:T(8,128)S(1)}, f32[3,4,128,128]{3,2,1,0:T(8,128)S(1)}) custom-call(s32[3]{0:T(128)S(1)} %add_add_fusion.1.where_ref, bf16[2,2,2048,512]{3,2,1,0:T(8,128)(2,1)} %kern_ref.3, bf16[2,2,2048,512]{3,2,1,0:T(8,128)(2,1)} %kern_ref.3, bf16[2,2,2048,512]{3,2,1,0:T(8,128)(2,1)} %kern_ref.3, bf16[2,2,2048,512]{3,2,1,0:T(8,128)(2,1)} %kern_ref.3), custom_call_target="tpu_custom_call" | custom-call | flops 1048576 | bytes 2097152 | tf_op jit(solution)/shard_map/pallas_call | solution.py:416
  10.1 5.1 %collective-permute-start.1 = (f32[3,4,128,128]{3,2,1,0:T(8,128)S(1)}, f32[3,4,128,128]{3,2,1,0:T(8,128)}, u32[]{:S(2)}, u32[]{:S(2)}) collective-permute-start(f32[3,4,128,128]{3,2,1,0:T(8,128)S(1)} %get-tuple-element.16), channel_id=1, source_target_pairs={{0,12},{4,8},{8,4},{12,0},{1,13},{5,9},{9,5},{13,1},{2,14},{6,10},... | collective-permute-start | bytes 2359304 | tf_op jit(solution)/shard_map/ppermute | solution.py:436
  15.9 2.0 convert_reduce_fusion
  19.5 8.7 %shard_map.145 = (f32[4,2,512,128]{3,2,1,0:T(8,128)S(1)}, f32[4,2,512,128]{3,2,1,0:T(8,128)S(1)}) custom-call(f32[1]{0:T(128)} %bitcast.1.offset_ref, f32[1,1,512,2048]{3,2,1,0:T(8,128)} %in_ref.1, bf16[8,512,256]{2,1,0:T(8,128)(2,1)} %constant.54.clone.high_ref, bf16[8,512,256]{2,1,0:T(8,128)(2,1)} %constant.55.clone.low_ref), custom_call_target="tpu_custom_call" | custom-call | flops 6442450944 | bytes 12582912 | tf_op jit(solution)/shard_map/pallas_call | solution.py:441
  28.2 1.4 copy-done.5
  29.6 1.9 broadcast_select_fusion.edge_ref
  31.5 2.3 collective-permute-done.1
  33.8 2.3 pad_maximum_fusion
  36.2 71.5 %all_to_all.20.in_ref = f32[4,2,512,128]{3,2,1,0:T(8,128)} all-to-all(f32[4,2,512,128]{3,2,1,0:T(8,128)S(1)} %get-tuple-element.14), channel_id=1, replica_groups=mesh['grp'=2,'pencil'=4,'depth'=2,'mem'=2] {'pencil'}, dimensions={0} | all-to-all | bytes 4194304 | tf_op jit(solution)/shard_map/all_to_all | solution.py:456
  107.7 3.7 %all-to-all-start = ((f32[4,2,512,128]{3,2,1,0:T(8,128)}), f32[4,2,512,128]{3,2,1,0:T(8,128)S(1)}, u32[]{:S(2)}, u32[]{:S(2)}) async-start(f32[4,2,512,128]{3,2,1,0:T(8,128)} %copy-done.5), calls=%async_computation | async-start | bytes 4194304 | tf_op jit(solution)/shard_map/all_to_all | solution.py:456
  111.5 1.6 copy-done.2
  113.1 1.0 copy-done.3
  114.2 12.9 %shard_map.147 = f32[2,4,2,256,128]{4,3,2,1,0:T(8,128)S(1)} custom-call(s32[3]{0:T(128)S(1)} %add_add_fusion.where_ref, f32[4,2,512,128]{3,2,1,0:T(8,128)S(1)} %copy-done.2, bf16[2,2,2048,512]{3,2,1,0:T(8,128)(2,1)} %kern_ref.3, f32[4,4,4,128,128]{4,3,2,1,0:T(8,128)} %bitcast.30, f32[2,16,128,128]{3,2,1,0:T(8,128)} %broadcast_select_fusion.edge_ref, ...), custom_call_target="tpu_custom_call" | custom-call | flops 1610612736 | bytes 16777216 | tf_op jit(solution)/shard_map/pallas_call | solution.py:494
  127.2 1.6 collective-permute-start.2
  128.8 22.2 %collective-permute-done.2 = f32[4,2,256,128]{3,2,1,0:T(8,128)S(1)} collective-permute-done((f32[4,2,256,128]{3,2,1,0:T(8,128)S(1)}, f32[4,2,256,128]{3,2,1,0:T(8,128)S(1)}, u32[]{:S(2)}, u32[]{:S(2)}) %collective-permute-start.2) | collective-permute-done | bytes 1048608 | tf_op jit(solution)/shard_map/ppermute | solution.py:528
  150.9 1.1 fusion.1
  152.0 6.7 %all-to-all-done.in_ref = f32[4,2,512,128]{3,2,1,0:T(8,128)S(1)} async-done(((f32[4,2,512,128]{3,2,1,0:T(8,128)}), f32[4,2,512,128]{3,2,1,0:T(8,128)S(1)}, u32[]{:S(2)}, u32[]{:S(2)}) %all-to-all-start) | async-done | bytes 2097184 | tf_op jit(solution)/shard_map/all_to_all | solution.py:456
  158.7 4.2 %all-to-all-start.2 = ((f32[4,2,256,128]{3,2,1,0:T(8,128)}), f32[4,2,256,128]{3,2,1,0:T(8,128)}, u32[]{:S(2)}, u32[]{:S(2)}) async-start(f32[4,2,256,128]{3,2,1,0:T(8,128)} %fusion.1), calls=%async_computation.2 | async-start | bytes 2097152 | tf_op jit(solution)/shard_map/all_to_all | solution.py:492
  162.9 1.0 copy-done.4
  164.0 10.9 %shard_map.148 = f32[2,4,2,256,128]{4,3,2,1,0:T(8,128)S(1)} custom-call(s32[3]{0:T(128)S(1)} %add_add_fusion.where_ref, f32[4,2,512,128]{3,2,1,0:T(8,128)S(1)} %all-to-all-done.in_ref, bf16[2,2,2048,512]{3,2,1,0:T(8,128)(2,1)} %kern_ref.3, f32[4,4,4,128,128]{4,3,2,1,0:T(8,128)} %bitcast.31, f32[2,16,128,128]{3,2,1,0:T(8,128)} %broadcast_select_fusion.edge_ref, ...), custom_call_target="tpu_custom_call" | custom-call | flops 1610612736 | bytes 16777216 | tf_op jit(solution)/shard_map/pallas_call | solution.py:494
  175.0 1.6 collective-permute-start.3
  176.6 22.6 %collective-permute-done.3 = f32[4,2,256,128]{3,2,1,0:T(8,128)S(1)} collective-permute-done((f32[4,2,256,128]{3,2,1,0:T(8,128)S(1)}, f32[4,2,256,128]{3,2,1,0:T(8,128)S(1)}, u32[]{:S(2)}, u32[]{:S(2)}) %collective-permute-start.3) | collective-permute-done | bytes 1048608 | tf_op jit(solution)/shard_map/ppermute | solution.py:528
  199.3 28.3 %all_to_all.21.refs_1_ = f32[4,2,256,128]{3,2,1,0:T(8,128)S(1)} all-to-all(f32[4,2,256,128]{3,2,1,0:T(8,128)S(1)} %fusion), channel_id=1, replica_groups=mesh['grp'=2,'pencil'=4,'depth'=2,'mem'=2] {'pencil'}, dimensions={0} | all-to-all | bytes 2097152 | tf_op jit(solution)/shard_map/all_to_all | solution.py:531
  227.6 5.7 %shard_map.149 = f32[1,256,2048]{2,1,0:T(8,128)} custom-call(f32[4,2,256,128]{3,2,1,0:T(8,128)} %all-to-all-done.2.refs_0_, f32[4,2,256,128]{3,2,1,0:T(8,128)S(1)} %all_to_all.21.refs_1_, bf16[8,512,256]{2,1,0:T(8,128)(2,1)S(1)} %copy-done.6, bf16[8,512,256]{2,1,0:T(8,128)(2,1)} %constant.63.clone.refs_3_), custom_call_target="tpu_custom_call" | custom-call | flops 3221225472 | bytes 8388608 | tf_op jit(solution)/shard_map/pallas_call | solution.py:534
  (32 shorter events, 2.1 us)
Async XLA Ops:
  6.5 12.3 %copy-start = (f32[8,1]{0,1:T(1,128)S(1)}, f32[8,1]{0,1:T(1,128)}, u32[]{:S(2)}) copy-start(f32[8,1]{0,1:T(1,128)} %param.16) | copy-start | bytes 100
  6.5 105.0 %all-gather.3.cloned.1.call-start = ((), (), s32[]{:S(2)}) async-start(), calls=%async_computation.4 | async-start | bytes 5242880 | tf_op jit(solution)/shard_map/all_gather | solution.py:469
  7.3 12.1 %copy-start.7 = (f32[2]{0:T(128)S(1)}, f32[2]{0:T(128)}, u32[]{:S(2)}) copy-start(f32[2]{0:T(128)} %constant.56.clone) | copy-start | bytes 28
  10.1 23.7 %collective-permute-start.1 = (f32[3,4,128,128]{3,2,1,0:T(8,128)S(1)}, f32[3,4,128,128]{3,2,1,0:T(8,128)}, u32[]{:S(2)}, u32[]{:S(2)}) collective-permute-start(f32[3,4,128,128]{3,2,1,0:T(8,128)S(1)} %get-tuple-element.16), channel_id=1, source_target_pairs={{0,12},{4,8},{8,4},{12,0},{1,13},{5,9},{9,5},{13,1},{2,14},{6,10},... | collective-permute-start | bytes 2359304 | tf_op jit(solution)/shard_map/ppermute | solution.py:436
  15.2 16.3 %collective-permute-start = (f32[1,4,128,128]{3,2,1,0:T(8,128)S(1)}, f32[1,4,128,128]{3,2,1,0:T(8,128)S(1)}, u32[]{:S(2)}, u32[]{:S(2)}) collective-permute-start(f32[1,4,128,128]{3,2,1,0:T(8,128)S(1)} %get-tuple-element.15), channel_id=1, source_target_pairs={{0,0},{4,12},{8,8},{12,4},{1,1},{5,13},{9,9},{13,5},{2,2},{6,14},{... | collective-permute-start | bytes 786440 | tf_op jit(solution)/shard_map/ppermute | solution.py:434
  28.2 1.4 copy-start.5
  107.7 3.8 %copy-start.1 = (f32[16,128,128]{2,1,0:T(8,128)S(1)}, f32[16,128,128]{2,1,0:T(8,128)}, u32[]{:S(2)}) copy-start(f32[16,128,128]{2,1,0:T(8,128)} %constant.57.clone.turns_ref.late_ref) | copy-start | bytes 3145732
  107.7 51.0 %all-to-all-start = ((f32[4,2,512,128]{3,2,1,0:T(8,128)}), f32[4,2,512,128]{3,2,1,0:T(8,128)S(1)}, u32[]{:S(2)}, u32[]{:S(2)}) async-start(f32[4,2,512,128]{3,2,1,0:T(8,128)} %copy-done.5), calls=%async_computation | async-start | bytes 4194304 | tf_op jit(solution)/shard_map/all_to_all | solution.py:456
  111.5 1.6 copy-start.2
  113.1 1.0 copy-start.3
  127.2 23.8 %collective-permute-start.2 = (f32[4,2,256,128]{3,2,1,0:T(8,128)S(1)}, f32[4,2,256,128]{3,2,1,0:T(8,128)S(1)}, u32[]{:S(2)}, u32[]{:S(2)}) collective-permute-start(f32[4,2,256,128]{3,2,1,0:T(8,128)S(1)} %slice_bitcast_fusion.2), channel_id=1, source_target_pairs={{0,2},{2,0},{1,3},{3,1},{4,6},{6,4},{5,7},{7,5},{8,10},{10,8},{9,1... | collective-permute-start | bytes 3145736 | tf_op jit(solution)/shard_map/ppermute | solution.py:528
  158.7 40.6 %all-to-all-start.2 = ((f32[4,2,256,128]{3,2,1,0:T(8,128)}), f32[4,2,256,128]{3,2,1,0:T(8,128)}, u32[]{:S(2)}, u32[]{:S(2)}) async-start(f32[4,2,256,128]{3,2,1,0:T(8,128)} %fusion.1), calls=%async_computation.2 | async-start | bytes 2097152 | tf_op jit(solution)/shard_map/all_to_all | solution.py:492
  162.9 1.0 copy-start.4
  175.0 52.6 %copy-start.6 = (bf16[8,512,256]{2,1,0:T(8,128)(2,1)S(1)}, bf16[8,512,256]{2,1,0:T(8,128)(2,1)}, u32[]{:S(2)}) copy-start(bf16[8,512,256]{2,1,0:T(8,128)(2,1)} %constant.62.clone.refs_2_) | copy-start | bytes 6291460
  175.0 24.2 %collective-permute-start.3 = (f32[4,2,256,128]{3,2,1,0:T(8,128)S(1)}, f32[4,2,256,128]{3,2,1,0:T(8,128)S(1)}, u32[]{:S(2)}, u32[]{:S(2)}) collective-permute-start(f32[4,2,256,128]{3,2,1,0:T(8,128)S(1)} %slice_bitcast_fusion), channel_id=1, source_target_pairs={{0,2},{2,0},{1,3},{3,1},{4,6},{6,4},{5,7},{7,5},{8,10},{10,8},{9,1... | collective-permute-start | bytes 3145736 | tf_op jit(solution)/shard_map/ppermute | solution.py:528
Sparse Core Ops, SparseCore 0:
  36.3 55.1 all-gather.2
